TPU v7x, 128 devices: a whole 4x4x4 slice. The times are simulated.
128 devices in a mesh: shard: 32 (over x, y, core), rep: 4 (over z).
Axes of the slice: x: 4, y: 4, z: 4, core: 2. Of those that a mesh axis runs over, the one named last changes fastest.
Arguments:
- embeddings: float32 [65536, 768], P(('shard', 'rep')), may hold values from -6 to 6
- destination: int32 [65536, 1], P(('shard', 'rep')), may hold values from 0 to 127; in each aligned block of 512 rows (0 to 511, 512 to 1023, ...) at most 8 rows name the same one
- labels: int32 [65536], P(('shard', 'rep')), may hold values from 0 to 127
- old_centroids: float32 [16384, 768], P(('shard', 'rep')), may hold values from -6 to 6
- codebook: float32 [128, 256, 6], P('rep'), may hold values from -6 to 6
Outputs:
- new_centroids: float32 [16384, 768], P(('shard', 'rep'))
- distortion: float32 [128, 131072], P('rep', 'shard')
Inputs may be any that keep to these rules, and one draw needn't show every extreme that they name: Among the rows of one owner, no destination is named more than 8 times, a bound that some block reaches.
All inputs are finite; a program needn't handle non-finite values.
Results may differ from a plain program's by a relative error of at most 0.0003.
Values sent between devices are 32-bit elements; how exact they have to be, the bound alone decides.
No kernel may reach another device: no remote copies, remote signals or barrier semaphores. Data moves between devices by JAX's collectives and lax.ppermute only.
A program may use at most 64 MiB of HBM per device.

v0:
```python
import jax
import jax.numpy as jnp
from jax import lax
from jax.sharding import PartitionSpec as P

prior_weight = 8.0


def positions(targets_row, owners):
    indicator = (targets_row[:, None] == jnp.arange(owners, dtype=jnp.int32)[None, :]).astype(
        jnp.int32
    )
    return jnp.sum((jnp.cumsum(indicator, axis=0) - 1) * indicator, axis=1)


def rebalance(block_rows, block_labels, previous):
    indicator = (
        block_labels[:, None] == jnp.arange(previous.shape[0], dtype=jnp.int32)[None, :]
    ).astype(jnp.float32)
    sums = jnp.dot(
        indicator.T, block_rows, precision=lax.Precision.HIGHEST, preferred_element_type=jnp.float32
    )
    counts = jnp.sum(indicator, axis=0)
    centroids = (prior_weight * previous + sums) / (prior_weight + counts)[:, None]
    residual = block_rows - jnp.dot(
        indicator, centroids, precision=lax.Precision.HIGHEST, preferred_element_type=jnp.float32
    )
    return (centroids, residual)


def distortion(residual, book):
    row_count = residual.shape[0]
    sub_count = book.shape[0]
    sub_dim = book.shape[2]
    block_width = max(1, min(sub_count, 32768 // row_count))
    while sub_count % block_width:
        block_width -= 1
    block_count = sub_count // block_width
    subvectors = residual.reshape(row_count, block_count, block_width, sub_dim).transpose(
        1, 0, 2, 3
    )
    book_blocks = book.reshape(block_count, block_width, book.shape[1], sub_dim)

    def block_distortion(operands):
        segment, codewords = operands
        inner_term = jnp.einsum("rmd,mkd->mrk", segment, codewords, precision=lax.Precision.HIGHEST)
        row_norms = jnp.sum(segment * segment, axis=-1).T
        word_norms = jnp.sum(codewords * codewords, axis=-1)
        return jnp.min(row_norms[:, :, None] - 2.0 * inner_term + word_norms[:, None, :], axis=2)

    result_blocks = lax.map(block_distortion, (subvectors, book_blocks))
    return result_blocks.reshape(sub_count, row_count)


def local(embeddings, destination, labels, old_centroids, codebook):
    n_shard = lax.axis_size("shard")
    n_rep = lax.axis_size("rep")
    owners = n_shard * n_rep
    row_count = embeddings.shape[0]
    feature = embeddings.shape[1]
    capacity = 2 * row_count // owners
    targets = destination[:, 0]
    slot_index = targets * capacity + positions(targets, owners)
    outgoing = jnp.zeros((owners * capacity, feature), jnp.float32).at[slot_index].set(embeddings)
    outgoing_labels = (
        jnp.full((owners * capacity,), -1.0, jnp.float32)
        .at[slot_index]
        .set(labels.astype(jnp.float32))
    )
    received, received_labels = (
        lax.all_to_all(outgoing, ("shard", "rep"), split_axis=0, concat_axis=0, tiled=True),
        lax.all_to_all(outgoing_labels, ("shard", "rep"), split_axis=0, concat_axis=0, tiled=True),
    )
    centroids, residual = rebalance(received, received_labels.astype(jnp.int32), old_centroids)
    regrouped = lax.all_to_all(residual, "rep", split_axis=1, concat_axis=0, tiled=True)
    scores = distortion(regrouped, codebook)
    return (centroids, scores)


def solution(mesh):
    placed = (
        P(("shard", "rep"), None),
        P(("shard", "rep"), None),
        P(("shard", "rep")),
        P(("shard", "rep"), None),
        P("rep", None, None),
    )
    return jax.shard_map(
        local,
        mesh=mesh,
        in_specs=placed,
        out_specs=(P(("shard", "rep"), None), P("rep", "shard")),
        check_vma=False,
    )
```

profile of v0, /device:TPU:1, one launch (start us, length us, event | category | flops | bytes accessed | tf_op | source)
XLA Modules:
  0.0 267.4 jit_solution(9541502256604349079)
XLA Ops:
  0.6 0.8 copy.21
  1.8 0.9 fusion.10
  2.7 0.7 compare_select_fusion
  3.4 0.7 convert_element_type.22
  4.1 2.4 scatter_custom_fusion
  6.5 0.7 all_to_all.26
  7.2 11.5 %all-to-all-start = ((f32[128,8,1]{1,2,0:T(1,128)}), f32[128,8,1]{1,2,0:T(1,128)S(1)}, u32[]{:S(2)}, u32[]{:S(2)}) async-start(f32[128,8,1]{1,2,0:T(1,128)} %bitcast.11), calls=%async_computation | async-start | bytes 131072 | tf_op jit(solution)/shard_map/all_to_all | solution.py:72
  18.7 4.9 %scatter_custom_fusion.1 = f32[1024,768]{1,0:T(8,128)} fusion(s32[512]{0:T(512)S(1)} %bitcast.63, f32[512,768]{1,0:T(8,128)} %param.7, f32[]{:T(128)} %constant.27.clone.1), kind=kCustom, calls=%fused_computation.14 | custom fusion | bytes 3146240 | tf_op jit(solution)/shard_map/scatter | solution.py:64
  23.6 4.7 %all-to-all-done = f32[128,8,1]{1,2,0:T(1,128)S(1)} async-done(((f32[128,8,1]{1,2,0:T(1,128)}), f32[128,8,1]{1,2,0:T(1,128)S(1)}, u32[]{:S(2)}, u32[]{:S(2)}) %all-to-all-start) | async-done | bytes 4128 | tf_op jit(solution)/shard_map/all_to_all | solution.py:72
  28.3 5.1 %all-to-all-start.1 = ((f32[128,8,768]{2,1,0:T(8,128)}), f32[128,8,768]{2,1,0:T(8,128)S(1)}, u32[]{:S(2)}, u32[]{:S(2)}) async-start(f32[128,8,768]{2,1,0:T(8,128)} %bitcast.54), calls=%async_computation.1 | async-start | bytes 6291456 | tf_op jit(solution)/shard_map/all_to_all | solution.py:71
  33.9 41.5 %all-to-all-done.1 = f32[128,8,768]{2,1,0:T(8,128)S(1)} async-done(((f32[128,8,768]{2,1,0:T(8,128)}), f32[128,8,768]{2,1,0:T(8,128)S(1)}, u32[]{:S(2)}, u32[]{:S(2)}) %all-to-all-start.1) | async-done | bytes 3145760 | tf_op jit(solution)/shard_map/all_to_all | solution.py:71
  75.5 2.4 copy.24
  77.8 2.6 fusion.9
  80.4 3.3 %convolution_subtract_fusion = f32[1024,768]{0,1:T(8,128)} fusion(f32[1024,768]{0,1:T(8,128)S(1)} %copy-done.1, f32[128,768]{1,0:T(8,128)S(1)} %fusion.9, s32[1024]{0:T(1024)S(1)} %convert_element_type.24), kind=kOutput, calls=%fused_computation.13 | convolution fusion | flops 1208877056 | bytes 6688768 | tf_op jit(solution)/shard_map/dot_general | solution.py:25
  83.7 3.9 %all-to-all-start.2 = ((f32[1024,4,192]{0,2,1:T(8,128)}), f32[1024,4,192]{0,2,1:T(8,128)S(1)}, u32[]{:S(2)}, u32[]{:S(2)}) async-start(f32[1024,4,192]{0,2,1:T(8,128)} %bitcast.56), calls=%async_computation.2 | async-start | bytes 6291456 | tf_op jit(solution)/shard_map/all_to_all | solution.py:75
  87.6 1.1 copy.26
  88.7 36.0 %all-to-all-done.2 = f32[1024,4,192]{0,2,1:T(8,128)S(1)} async-done(((f32[1024,4,192]{0,2,1:T(8,128)}), f32[1024,4,192]{0,2,1:T(8,128)S(1)}, u32[]{:S(2)}, u32[]{:S(2)}) %all-to-all-start.2) | async-done | bytes 3145760 | tf_op jit(solution)/shard_map/all_to_all | solution.py:75
  124.7 1.7 copy-done
  126.3 3.9 %copy.25 = f32[4,1024,192]{1,0,2:T(4,128)S(1)} copy(f32[4,1024,192]{1,2,0:T(8,128)} %bitcast.55) | data formatting | bytes 6291456 | tf_op jit(solution)/shard_map/all_to_all | solution.py:75
  130.3 3.5 %reshape.52 = f32[4096,4,8,6]{0,3,2,1:T(8,128)} reshape(f32[4,1024,192]{1,0,2:T(4,128)S(1)} %copy.25) | data formatting | bytes 6291456 | tf_op jit(solution)/shard_map/reshape | solution.py:39
  133.7 133.6 %while.10 = (s32[]{:T(128)}, f32[4,8,4096]{2,1,0:T(8,128)}, f32[4,4096,8,6]{1,3,2,0:T(8,128)}, f32[4,8,256,6]{2,3,1,0:T(8,128)S(1)}, s32[]{:T(128)}) while((s32[]{:T(128)}, f32[4,8,4096]{2,1,0:T(8,128)}, f32[4,4096,8,6]{1,3,2,0:T(8,128)}, f32[4,8,256,6]{2,3,1,0:T(8,128)S(1)}, s32[]{:T(128)}) %tuple.26), condition=%wide.region_10.11_spmd, body=%wide.region_6.0_spmd.sunk | while | flops 637884416 | bytes 2623045 | solution.py:51
  133.7 1.6 fusion.27
  135.4 31.1 %add_reduce_fusion.2 = f32[8,4096]{1,0:T(8,128)S(1)} fusion(f32[8,256]{1,0:T(8,128)S(1)} %fusion.26, f32[8,4096]{1,0:T(8,128)S(1)} %bitcast.57, f32[4,4096,8,6]{1,3,2,0:T(8,128)} %get-tuple-element.70, s32[]{:T(128)} %get-tuple-element.63, f32[4,8,256,6]{2,3,1,0:T(8,128)S(1)} %get-tuple-element.71), kind=kOutput, calls=%fused_computation.2.clone.1 | convolution fusion | flops 637501440 | bytes 1385472 | tf_op jit(solution)/shard_map/while/body/eval_jaxpr/rmd,mkd->mrk/dot_general | solution.py:46
  166.5 0.7 bitcast_dynamic-update-slice_fusion.2
  167.1 1.6 fusion.27
  168.8 31.1 %add_reduce_fusion.2 = f32[8,4096]{1,0:T(8,128)S(1)} fusion(f32[8,256]{1,0:T(8,128)S(1)} %fusion.26, f32[8,4096]{1,0:T(8,128)S(1)} %bitcast.57, f32[4,4096,8,6]{1,3,2,0:T(8,128)} %get-tuple-element.70, s32[]{:T(128)} %get-tuple-element.63, f32[4,8,256,6]{2,3,1,0:T(8,128)S(1)} %get-tuple-element.71), kind=kOutput, calls=%fused_computation.2.clone.1 | convolution fusion | flops 637501440 | bytes 1385472 | tf_op jit(solution)/shard_map/while/body/eval_jaxpr/rmd,mkd->mrk/dot_general | solution.py:46
  199.9 0.7 bitcast_dynamic-update-slice_fusion.2
  200.6 1.6 fusion.27
  202.2 31.1 %add_reduce_fusion.2 = f32[8,4096]{1,0:T(8,128)S(1)} fusion(f32[8,256]{1,0:T(8,128)S(1)} %fusion.26, f32[8,4096]{1,0:T(8,128)S(1)} %bitcast.57, f32[4,4096,8,6]{1,3,2,0:T(8,128)} %get-tuple-element.70, s32[]{:T(128)} %get-tuple-element.63, f32[4,8,256,6]{2,3,1,0:T(8,128)S(1)} %get-tuple-element.71), kind=kOutput, calls=%fused_computation.2.clone.1 | convolution fusion | flops 637501440 | bytes 1385472 | tf_op jit(solution)/shard_map/while/body/eval_jaxpr/rmd,mkd->mrk/dot_general | solution.py:46
  233.3 0.7 bitcast_dynamic-update-slice_fusion.2
  234.0 1.6 fusion.27
  235.6 31.1 %add_reduce_fusion.2 = f32[8,4096]{1,0:T(8,128)S(1)} fusion(f32[8,256]{1,0:T(8,128)S(1)} %fusion.26, f32[8,4096]{1,0:T(8,128)S(1)} %bitcast.57, f32[4,4096,8,6]{1,3,2,0:T(8,128)} %get-tuple-element.70, s32[]{:T(128)} %get-tuple-element.63, f32[4,8,256,6]{2,3,1,0:T(8,128)S(1)} %get-tuple-element.71), kind=kOutput, calls=%fused_computation.2.clone.1 | convolution fusion | flops 637501440 | bytes 1385472 | tf_op jit(solution)/shard_map/while/body/eval_jaxpr/rmd,mkd->mrk/dot_general | solution.py:46
  (21 shorter events, 1.6 us)
Async XLA Ops:
  7.2 21.1 %all-to-all-start = ((f32[128,8,1]{1,2,0:T(1,128)}), f32[128,8,1]{1,2,0:T(1,128)S(1)}, u32[]{:S(2)}, u32[]{:S(2)}) async-start(f32[128,8,1]{1,2,0:T(1,128)} %bitcast.11), calls=%async_computation | async-start | bytes 131072 | tf_op jit(solution)/shard_map/all_to_all | solution.py:72
  28.3 47.1 %all-to-all-start.1 = ((f32[128,8,768]{2,1,0:T(8,128)}), f32[128,8,768]{2,1,0:T(8,128)S(1)}, u32[]{:S(2)}, u32[]{:S(2)}) async-start(f32[128,8,768]{2,1,0:T(8,128)} %bitcast.54), calls=%async_computation.1 | async-start | bytes 6291456 | tf_op jit(solution)/shard_map/all_to_all | solution.py:71
  77.8 2.6 copy-start.1
  80.4 3.3 %copy-start.2 = (f32[128,768]{1,0:T(8,128)}, f32[128,768]{1,0:T(8,128)S(1)}, u32[]{:S(2)}) copy-start(f32[128,768]{1,0:T(8,128)S(1)} %fusion.9) | copy-start | bytes 1179652
  83.7 41.0 %all-to-all-start.2 = ((f32[1024,4,192]{0,2,1:T(8,128)}), f32[1024,4,192]{0,2,1:T(8,128)S(1)}, u32[]{:S(2)}, u32[]{:S(2)}) async-start(f32[1024,4,192]{0,2,1:T(8,128)} %bitcast.56), calls=%async_computation.2 | async-start | bytes 6291456 | tf_op jit(solution)/shard_map/all_to_all | solution.py:75
  124.7 1.7 copy-start
where the time goes:
time: 268 us; the launch traced here: 267 us
  matrix products  130 us (49%)
  waiting for transfers between devices  82.2 us (31%)
  local copies, waits for them, and re-layouts  24.1 us (9%)
  starting transfers between devices  20.4 us (8%)
  other arithmetic  9.42 us (4%)
    dot_general x4, matrix products, block_distortion(): jnp.einsum('rmd,mkd->mrk', segment, codewords, precision=lax.Precision.HI...  124 us
    all_to_all x1, waiting for transfers between devices, local(): lax.all_to_all(outgoing, ('shard', 'rep'), split_axis=0, concat_axis=0, t...  41.5 us
    all_to_all x1, waiting for transfers between devices, local(): lax.all_to_all(residual, 'rep', split_axis=1, concat_axis=0, tiled=True)  36 us
    all_to_all x1, starting transfers between devices, local(): lax.all_to_all(outgoing_labels, ('shard', 'rep'), split_axis=0, concat_ax...  11.5 us
    reduce_sum x4, other arithmetic, block_distortion(): row_norms = jnp.sum(segment * segment, axis=-1).T  6.3 us
  transfers between devices with their start and end apart: 3, of which 3 were waited for; matrix products, arithmetic and copies ran while one was open for 2% of the time, Pallas kernels for 0%

commit v1 on v0

v1 whole, which is shorter than its diff:
```python
import functools
import jax
import jax.numpy as jnp
from jax import lax
from jax.experimental import pallas as pl
from jax.experimental.pallas import tpu as pltpu
from jax.sharding import PartitionSpec as P

prior_weight = 8.0
F32 = jnp.float32
BF16 = jnp.bfloat16
VMEM = pl.BlockSpec(memory_space=pltpu.VMEM)
SMEM = pl.BlockSpec(memory_space=pltpu.SMEM)
LIMIT = 56 * 2**20
MSG = 49


def split3(x):
    first = x.astype(BF16)
    rest = x - first.astype(F32)
    second = rest.astype(BF16)
    third = (rest - second.astype(F32)).astype(BF16)
    return first, second, third


def iota(shape, dim):
    return lax.broadcasted_iota(jnp.int32, shape, dim)


def dot(a, b):
    return jnp.dot(a, b, preferred_element_type=F32)


def pack_kernel(dest_ref, label_ref, rows_ref, out_ref, a_ref, b_ref):
    dest = dest_ref[...]
    named = (iota((128, 512), 0) == dest).astype(F32)
    earlier = (iota((512, 512), 0) < iota((512, 512), 1)).astype(BF16)
    before = dot(named.astype(BF16), earlier)
    slot = dest * 8 + jnp.sum(named * before, axis=0, keepdims=True).astype(jnp.int32)

    group = (iota((32, 512), 0) == slot // 32).astype(F32)
    within = (iota((128, 512), 0) == slot % 32).astype(BF16)
    labels = group * (label_ref[...] + 1).astype(F32)
    label_rows = lax.dot_general(
        labels.astype(BF16), within, (((1,), (1,)), ((), ())), preferred_element_type=F32
    ) - 1.0
    for quarter in range(4):
        out_ref[pl.ds(MSG * quarter + 48, 32, stride=4 * MSG), :] = label_rows

    low = iota((512, 128), 1) < 64
    tile = [rows_ref[:, 128 * i : 128 * i + 128] for i in range(6)]
    wide = [
        tile[0],
        pltpu.roll(jnp.where(low, tile[2], tile[1]), 64, 1),
        tile[3],
        pltpu.roll(jnp.where(low, tile[5], tile[4]), 64, 1),
    ]
    narrow = [jnp.where(low, tile[1], tile[2]), jnp.where(low, tile[4], tile[5])]
    for i, block in enumerate(wide + narrow):
        for piece, part in enumerate(split3(block)):
            a_ref[512 * piece : 512 * piece + 512, 128 * i : 128 * i + 128] = part

    for half in range(2):
        pick = (iota((512, 512), 0) + 512 * half == slot).astype(BF16)
        b_ref[...] = (
            dot(pick, a_ref[0:512, :]) + dot(pick, a_ref[512:1024, :]) + dot(pick, a_ref[1024:1536, :])
        )
        lower = iota((8, 128), 1) < 64
        for s in range(16):
            for quarter in range(4):
                base = MSG * (4 * (16 * half + s) + quarter)
                out_ref[pl.ds(base, 32), :] = b_ref[32 * s : 32 * s + 32, 128 * quarter : 128 * quarter + 128]
                lanes = 512 + 128 * (quarter // 2)
                for pair in range(2):
                    one = b_ref[32 * s + 8 * pair : 32 * s + 8 * pair + 8, lanes : lanes + 128]
                    two = b_ref[32 * s + 8 * pair + 16 : 32 * s + 8 * pair + 24, lanes : lanes + 128]
                    if quarter % 2 == 0:
                        both = jnp.where(lower, one, pltpu.roll(two, 64, 1))
                    else:
                        both = jnp.where(lower, pltpu.roll(one, 64, 1), two)
                    out_ref[pl.ds(base + 32 + 8 * pair, 8), :] = both


def quarters_kernel(rep_ref, old_ref, own_ref, one_ref, two_ref, three_ref):
    rep = rep_ref[0]
    low = iota((128, 128), 1) < 64
    tile = [old_ref[:, 128 * i : 128 * i + 128] for i in range(6)]
    wide = [
        tile[0],
        pltpu.roll(jnp.where(low, tile[2], tile[1]), 64, 1),
        tile[3],
        pltpu.roll(jnp.where(low, tile[5], tile[4]), 64, 1),
    ]
    narrow = [tile[1], pltpu.roll(tile[2], 64, 1), tile[4], pltpu.roll(tile[5], 64, 1)]
    for step, ref in enumerate((own_ref, one_ref, two_ref, three_ref)):
        which = lax.rem(rep + step, 4)
        for start, choice in ((0, wide), (128, narrow)):
            ref[:, start : start + 128] = jnp.where(
                which == 0,
                choice[0],
                jnp.where(which == 1, choice[1], jnp.where(which == 2, choice[2], choice[3])),
            )


def book_kernel(book_ref, out_ref):
    row = iota((256, 256), 0)
    for g in range(4):
        words = book_ref[:, 8 * g : 8 * g + 8, :].reshape(48, 256)
        norm = jnp.sum((words * words).reshape(6, 8, 256), axis=0)
        first, second, third = (part.astype(F32) for part in split3(-2.0 * words))
        n1, n2, n3 = (part.astype(F32) for part in split3(norm))
        stack = jnp.concatenate([first, second, first, second, first], axis=0)
        for m in range(8):
            mine = jnp.where(iota((240, 256), 0) % 8 == m, stack, 0.0)
            tail_row = iota((16, 256), 0)
            tail = jnp.where(
                tail_row == 0,
                n1[m : m + 1],
                jnp.where(tail_row == 1, n2[m : m + 1], jnp.where(tail_row == 2, n3[m : m + 1], 0.0)),
            )
            out_ref[8 * g + m] = jnp.concatenate([mine, tail], axis=0).T.astype(BF16)


def centroid_kernel(rep_ref, got_ref, own_ref, one_ref, two_ref, three_ref, cent_ref, turned_ref, lab_ref):
    rep = rep_ref[0]
    lab = got_ref[pl.ds(48, 128, stride=MSG), :].astype(BF16)
    spread = (iota((128, 512), 0) == (iota((128, 512), 1) // 128) * 8 + iota((128, 512), 1) % 8).astype(BF16)
    moved = dot(lab, spread)
    keep = iota((128, 512), 0) % 16 == (iota((128, 512), 1) % 128) // 8
    lab_rows = jnp.sum(jnp.where(keep, moved, 0.0).reshape(8, 16, 512), axis=1)
    lab_ref[...] = lab_rows

    posting = iota((128, 128), 0).astype(F32)
    low = iota((128, 128), 1) < 64
    for pair in range(2):
        sums = [jnp.zeros((128, 256), F32), jnp.zeros((128, 256), F32)]
        counts = [jnp.zeros((128, 128), F32), jnp.zeros((128, 128), F32)]
        for c in range(8):
            senders = range(16 * c, 16 * c + 16)
            narrow = jnp.concatenate([got_ref[pl.ds(MSG * q + 32 + 8 * pair, 8), :] for q in senders], axis=0)
            narrow_parts = split3(narrow)
            narrow_turned = narrow.T
            for k in range(2):
                r = pair + 2 * k
                wide = jnp.concatenate([got_ref[pl.ds(MSG * q + 8 * r, 8), :] for q in senders], axis=0)
                hot = (posting == lab_rows[c : c + 1, 128 * r : 128 * r + 128]).astype(F32)
                counts[k] += hot
                hot = hot.astype(BF16)
                for part, other in zip(split3(wide), narrow_parts):
                    sums[k] += dot(hot, jnp.concatenate([part, other], axis=1))
                turned_ref[8 * r + c, 0:128, :] = wide.T
                turned_ref[8 * r + c, 128:192, :] = narrow_turned[64 * k : 64 * k + 64]
        for k in range(2):
            r = pair + 2 * k
            step = lax.rem(rep - r + 4, 4)
            weight = prior_weight + jnp.sum(counts[k], axis=1, keepdims=True)
            for start in (0, 128):
                total = sums[k][:, start : start + 128]
                if start and k:
                    total = pltpu.roll(total, 64, 1)
                olds = [ref[:, start : start + 128] for ref in (own_ref, one_ref, two_ref, three_ref)]
                old = jnp.where(
                    step == 0, olds[0], jnp.where(step == 1, olds[1], jnp.where(step == 2, olds[2], olds[3]))
                )
                new = (prior_weight * old + total) / weight
                if start:
                    new = jnp.where(low, new, 0.0)
                cent_ref[r, :, start : start + 128] = new


def score_kernel(turned_ref, cent_ref, lab_ref, book_ref, out_ref, flip_ref, cent3_ref, res_ref, norm_ref):
    for r in range(4):
        flip_ref[0:128, :] = cent_ref[r, :, 0:128].T
        flip_ref[128:256, :] = cent_ref[r, :, 128:256].T
        for g in range(4):
            for t in range(6):
                rows = flip_ref[pl.ds(48 * g + t, 8, stride=6), :]
                for piece, part in enumerate(split3(rows)):
                    cent3_ref[4 * r + g, 48 * piece + 8 * t : 48 * piece + 8 * t + 8, :] = part.astype(F32)
    ones = jnp.where(iota((16, 1024), 0) < 3, 1.0, 0.0).astype(BF16)
    res_ref[0, 240:256, :] = ones
    res_ref[1, 240:256, :] = ones

    def prepare(i, buffer):
        r = i // 4
        g = i % 4
        labs = lab_ref[:, pl.ds(pl.multiple_of(128 * r, 128), 128)]
        posting = iota((128, 128), 0).astype(F32)
        hot = jnp.concatenate([(posting == labs[c : c + 1]).astype(BF16) for c in range(8)], axis=1)
        part = dot(cent3_ref[i].astype(BF16), hot)
        near = part[0:48] + part[48:96] + part[96:144]
        rows = jnp.concatenate(
            [
                jnp.concatenate(
                    [turned_ref[8 * r + c, pl.ds(48 * g + t, 8, stride=6), :] for c in range(8)], axis=1
                )
                for t in range(6)
            ],
            axis=0,
        )
        res = rows - near
        norm_ref[buffer] = jnp.sum((res * res).reshape(6, 8, 1024), axis=0)
        first, second, third = split3(res)
        res_ref[buffer, 0:48, :] = first
        res_ref[buffer, 48:96, :] = first
        res_ref[buffer, 96:144, :] = second
        res_ref[buffer, 144:192, :] = second
        res_ref[buffer, 192:240, :] = third

    def score(i, buffer):
        r = i // 4
        g = i % 4
        right = res_ref[buffer]
        best = []
        for m in range(8):
            value = dot(book_ref[8 * g + m], right)
            value = jnp.min(value.reshape(32, 8, 1024), axis=0)
            best.append(jnp.min(value, axis=0, keepdims=True))
        out_ref[pl.ds(pl.multiple_of(8 * g, 8), 8), pl.ds(pl.multiple_of(1024 * r, 1024), 1024)] = (
            jnp.concatenate(best, axis=0) + norm_ref[buffer]
        )

    prepare(0, 0)

    def step(i, carry):
        score(i, i % 2)
        prepare(jnp.minimum(i + 1, 15), (i + 1) % 2)
        return carry

    lax.fori_loop(0, 16, step, 0)


def join_kernel(got_ref, out_ref):
    low = iota((128, 128), 1) < 64
    for half in range(2):
        wide0, narrow0 = got_ref[2 * half, :, 0:128], got_ref[2 * half, :, 128:256]
        wide1, narrow1 = got_ref[2 * half + 1, :, 0:128], got_ref[2 * half + 1, :, 128:256]
        turned = pltpu.roll(wide1, 64, 1)
        at = 384 * half
        out_ref[:, at : at + 128] = wide0
        out_ref[:, at + 128 : at + 256] = jnp.where(low, narrow0, turned)
        out_ref[:, at + 256 : at + 384] = jnp.where(low, turned, pltpu.roll(narrow1, 64, 1))


def call(kernel, out_shape, specs, scratch=(), flops=0, moved=0):
    many = isinstance(out_shape, (tuple, list))
    return pl.pallas_call(
        kernel,
        out_shape=out_shape,
        in_specs=specs,
        out_specs=[VMEM] * len(out_shape) if many else VMEM,
        scratch_shapes=scratch,
        compiler_params=pltpu.CompilerParams(vmem_limit_bytes=LIMIT),
        cost_estimate=pl.CostEstimate(flops=flops, bytes_accessed=moved, transcendentals=0),
    )


def shape(*dims, dtype=F32):
    return jax.ShapeDtypeStruct(dims, dtype)


def local(embeddings, destination, labels, old_centroids, codebook):
    rep = lax.axis_index("rep").astype(jnp.int32).reshape(1)
    outgoing = call(
        pack_kernel,
        shape(128 * MSG, 128),
        [VMEM] * 3,
        [pltpu.VMEM((1536, 768), BF16), pltpu.VMEM((512, 768), F32)],
        flops=2 * 1024 * 512 * 768 * 3,
        moved=5 * 2**20,
    )(destination.reshape(1, 512), labels.reshape(1, 512), embeddings)
    received = lax.all_to_all(
        outgoing.reshape(128, 1, MSG * 128), ("shard", "rep"), split_axis=0, concat_axis=0, tiled=True
    ).reshape(128 * MSG, 128)

    quarters = call(
        quarters_kernel, [shape(128, 256)] * 4, [SMEM, VMEM], flops=2**20, moved=2**20
    )(rep, old_centroids)
    olds = [quarters[0]]
    for step in (1, 2, 3):
        olds.append(lax.ppermute(quarters[step], "rep", [(i, (i + step) % 4) for i in range(4)]))
    book = call(
        book_kernel, shape(32, 256, 256, dtype=BF16), [VMEM], flops=2**28, moved=5 * 2**20
    )(jnp.transpose(codebook, (2, 0, 1)))

    cents, turned, lab_rows = call(
        centroid_kernel,
        [shape(4, 128, 256), shape(32, 192, 128), shape(8, 512)],
        [SMEM] + [VMEM] * 5,
        flops=2 * 128 * 4096 * 256 * 3,
        moved=7 * 2**20,
    )(rep, received, *olds)
    returned = lax.all_to_all(cents, "rep", split_axis=0, concat_axis=0, tiled=True)
    scores = call(
        score_kernel,
        shape(32, 4096),
        [VMEM] * 4,
        [
            pltpu.VMEM((256, 128), F32),
            pltpu.VMEM((16, 144, 128), F32),
            pltpu.VMEM((2, 256, 1024), BF16),
            pltpu.VMEM((2, 8, 1024), F32),
        ],
        flops=2 * 131072 * 256 * 256,
        moved=8 * 2**20,
    )(turned, cents, lab_rows, book)
    centroids = call(join_kernel, shape(128, 768), [VMEM], flops=2**18, moved=2**20)(returned)
    return (centroids, scores)


def solution(mesh):
    placed = (
        P(("shard", "rep"), None),
        P(("shard", "rep"), None),
        P(("shard", "rep")),
        P(("shard", "rep"), None),
        P("rep", None, None),
    )
    return jax.shard_map(
        local,
        mesh=mesh,
        in_specs=placed,
        out_specs=(P(("shard", "rep"), None), P("rep", "shard")),
        check_vma=False,
    )
```

time: 268 us -> 102 us (0.38)
  matrix products: 130 us -> 0 us
  waiting for transfers between devices: 82.2 us -> 32.5 us
  Pallas kernels: 0 us -> 45.8 us
  local copies, waits for them, and re-layouts: 24.1 us -> 2.52 us
  other arithmetic: 9.42 us -> 0 us
    dot_general x6 -> x0, matrix products: 130 us -> none  [the longest x4 124 us: block_distortion(): jnp.einsum('rmd,mkd->mrk', segment, codewords, precision=lax.Precision.HI...]
    all_to_all x3 -> x2, waiting for transfers between devices: 82.2 us -> 0.01 us  [the longest x1 0.01 us: local(): lax.all_to_all(outgoing.reshape(128, 1, MSG * 128), ('shard', 'rep'), spl...]
    pallas_call x0 -> x6, Pallas kernels: none -> 45.8 us  [the longest x1 26.2 us: local(): call(score_kernel, shape(32, 4096), [VMEM] * 4, [pltpu.VMEM((256, 128), F...]
    ppermute x0 -> x3, waiting for transfers between devices: none -> 32.5 us  [local(): lax.ppermute(quarters[step], 'rep', [(i, (i + step) % 4) for i in range(4)])]
    reduce_sum x10 -> x0, other arithmetic: 7.55 us -> none  [the longest x4 6.3 us: block_distortion(): row_norms = jnp.sum(segment * segment, axis=-1).T]
    scatter x2 -> x0, local copies, waits for them, and re-layouts: 7.36 us -> none  [the longest x1 4.92 us: local(): jnp.zeros((owners * capacity, feature), jnp.float32).at[slot_index]]
    all_to_all x3 -> x0, local copies, waits for them, and re-layouts: 6.99 us -> none  [the longest x1 3.91 us: local(): lax.all_to_all(residual, 'rep', split_axis=1, concat_axis=0, tiled=True)]
    all_to_all x3 -> x2, starting transfers between devices: 20.4 us -> 15 us  [the longest x1 11.5 us: local(): lax.all_to_all(outgoing.reshape(128, 1, MSG * 128), ('shard', 'rep'), spl...]
  transfers between devices with their start and end apart: 3 -> 5, of which waited for: 3 -> 2; matrix products, arithmetic and copies ran while one was open for 2% -> 0% of each run, Pallas kernels for 0% -> 32%
where the time goes in v1:
time: 102 us
  Pallas kernels  45.8 us (45%)
  waiting for transfers between devices  32.5 us (32%)
  starting transfers between devices  20.3 us (20%)
  local copies, waits for them, and re-layouts  2.52 us (2%)
    ppermute x3, waiting for transfers between devices, local(): lax.ppermute(quarters[step], 'rep', [(i, (i + step) % 4) for i in range(4)])  32.5 us
    pallas_call x1, Pallas kernels, local(): call(score_kernel, shape(32, 4096), [VMEM] * 4, [pltpu.VMEM((256, 128), F...  26.2 us
    all_to_all x1, starting transfers between devices, local(): lax.all_to_all(outgoing.reshape(128, 1, MSG * 128), ('shard', 'rep'), spl...  11.5 us
    pallas_call x1, Pallas kernels, local(): call(pack_kernel, shape(128 * MSG, 128), [VMEM] * 3, [pltpu.VMEM((1536, 7...  6.48 us
    ppermute x3, starting transfers between devices, local(): lax.ppermute(quarters[step], 'rep', [(i, (i + step) % 4) for i in range(4)])  5.35 us
    pallas_call x1, Pallas kernels, local(): call(centroid_kernel, [shape(4, 128, 256), shape(32, 192, 128), shape(8,...  5.08 us
    pallas_call x1, Pallas kernels, local(): call(book_kernel, shape(32, 256, 256, dtype=BF16), [VMEM], flops=2 ** 28,...  4.14 us
    all_to_all x1, starting transfers between devices, local(): lax.all_to_all(cents, 'rep', split_axis=0, concat_axis=0, tiled=True)  3.47 us
  transfers between devices with their start and end apart: 5, of which 2 were waited for; matrix products, arithmetic and copies ran while one was open for 0% of the time, Pallas kernels for 32%

profile of v1, /device:TPU:1, one launch (start us, length us, event | category | flops | bytes accessed | tf_op | source)
XLA Modules:
  0.0 101.8 jit_solution(1915420965317657757)
XLA Ops:
  0.6 6.5 %shard_map.68 = f32[6272,128]{1,0:T(8,128)} custom-call(s32[1,512]{1,0:T(1,128)} %bitcast.9, s32[1,512]{1,0:T(1,128)} %bitcast.10, f32[512,768]{1,0:T(8,128)} %rows_ref.1), custom_call_target="tpu_custom_call" | custom-call | flops 2415919104 | bytes 5242880 | tf_op jit(solution)/shard_map/pallas_call | solution.py:264
  7.1 11.5 %all-to-all-start = ((f32[128,1,6272]{2,1,0:T(1,128)}), f32[128,1,6272]{2,1,0:T(1,128)S(1)}, u32[]{:S(2)}, u32[]{:S(2)}) async-start(f32[128,1,6272]{2,1,0:T(1,128)} %bitcast.7), calls=%async_computation | async-start | bytes 6422528 | tf_op jit(solution)/shard_map/all_to_all | solution.py:272
  18.6 1.9 %shard_map.69 = (f32[128,256]{1,0:T(8,128)}, f32[128,256]{1,0:T(8,128)}, f32[128,256]{1,0:T(8,128)}, f32[128,256]{1,0:T(8,128)}) custom-call(s32[1]{0:T(128)} %bitcast.rep_ref, f32[128,768]{1,0:T(8,128)} %old_ref.1), custom_call_target="tpu_custom_call" | custom-call | flops 1048576 | bytes 1048576 | tf_op jit(solution)/shard_map/pallas_call | solution.py:276
  20.6 1.5 %collective-permute-start = (f32[128,256]{1,0:T(8,128)}, f32[128,256]{1,0:T(8,128)S(1)}, u32[]{:S(2)}, u32[]{:S(2)}) collective-permute-start(f32[128,256]{1,0:T(8,128)} %get-tuple-element.10), channel_id=1, source_target_pairs={{0,1},{1,2},{2,3},{3,0},{4,5},{5,6},{6,7},{7,4},{8,9},{9,10},{10,1... | collective-permute-start | bytes 393224 | tf_op jit(solution)/shard_map/ppermute | solution.py:281
  22.1 2.9 %collective-permute-start.1 = (f32[128,256]{1,0:T(8,128)}, f32[128,256]{1,0:T(8,128)S(1)}, u32[]{:S(2)}, u32[]{:S(2)}) collective-permute-start(f32[128,256]{1,0:T(8,128)} %get-tuple-element.11), channel_id=1, source_target_pairs={{0,2},{1,3},{2,0},{3,1},{4,6},{5,7},{6,4},{7,5},{8,10},{9,11},{10,... | collective-permute-start | bytes 393224 | tf_op jit(solution)/shard_map/ppermute | solution.py:281
  25.0 0.9 collective-permute-start.2
  25.9 4.1 %shard_map.72.book_ref = bf16[32,256,256]{2,1,0:T(8,128)(2,1)} custom-call(f32[6,32,256]{2,1,0:T(8,128)} %bitcast.8), custom_call_target="tpu_custom_call" | custom-call | flops 268435456 | bytes 5242880 | tf_op jit(solution)/shard_map/pallas_call | solution.py:282
  30.1 29.2 %collective-permute-done.one_ref = f32[128,256]{1,0:T(8,128)S(1)} collective-permute-done((f32[128,256]{1,0:T(8,128)}, f32[128,256]{1,0:T(8,128)S(1)}, u32[]{:S(2)}, u32[]{:S(2)}) %collective-permute-start) | collective-permute-done | bytes 131104 | tf_op jit(solution)/shard_map/ppermute | solution.py:281
  59.3 0.0 copy-start.2
  59.3 3.3 %collective-permute-done.1.two_ref = f32[128,256]{1,0:T(8,128)S(1)} collective-permute-done((f32[128,256]{1,0:T(8,128)}, f32[128,256]{1,0:T(8,128)S(1)}, u32[]{:S(2)}, u32[]{:S(2)}) %collective-permute-start.1) | collective-permute-done | bytes 131104 | tf_op jit(solution)/shard_map/ppermute | solution.py:281
  62.6 0.0 copy-start.3
  62.6 0.0 collective-permute-done.2.three_ref
  62.6 0.0 all-to-all-done
  62.6 0.0 copy-start
  62.6 0.0 copy-done.2
  62.6 0.6 copy-done.3
  63.2 1.1 %copy-done = f32[128,1,6272]{2,1,0:T(1,128)} copy-done((f32[128,1,6272]{2,1,0:T(1,128)}, f32[128,1,6272]{2,1,0:T(1,128)S(1)}, u32[]{:S(2)}) %copy-start) | copy-done | bytes 3211288
  64.3 5.1 %shard_map.70 = (f32[4,128,256]{2,1,0:T(8,128)}, f32[32,192,128]{2,1,0:T(8,128)}, f32[8,512]{1,0:T(8,128)}) custom-call(s32[1]{0:T(128)} %bitcast.rep_ref, f32[6272,128]{1,0:T(8,128)} %bitcast.6, f32[128,256]{1,0:T(8,128)} %get-tuple-element.9.own_ref, f32[128,256]{1,0:T(8,128)} %copy-done.2, f32[128,256]{1,0:T(8,128)} %copy-done.3, ...), custom_call_target="tpu_custom_call" | custom-call | flops 805306368 | bytes 7340032 | tf_op jit(solution)/shard_map/pallas_call | solution.py:286
  69.4 3.5 %all-to-all-start.1 = ((f32[4,128,256]{2,1,0:T(8,128)}), f32[4,128,256]{2,1,0:T(8,128)S(1)}, u32[]{:S(2)}, u32[]{:S(2)}) async-start(f32[4,128,256]{2,1,0:T(8,128)} %get-tuple-element.13.cent_ref), calls=%async_computation.1 | async-start | bytes 1048576 | tf_op jit(solution)/shard_map/all_to_all | solution.py:293
  72.9 26.2 %shard_map.73 = f32[32,4096]{1,0:T(8,128)} custom-call(f32[32,192,128]{2,1,0:T(8,128)} %get-tuple-element.14.turned_ref, f32[4,128,256]{2,1,0:T(8,128)} %get-tuple-element.13.cent_ref, f32[8,512]{1,0:T(8,128)} %get-tuple-element.15.lab_ref, bf16[32,256,256]{2,1,0:T(8,128)(2,1)} %shard_map.72.book_ref), custom_call_target="tpu_custom_call" | custom-call | flops 17179869184 | bytes 8388608 | tf_op jit(solution)/shard_map/pallas_call | solution.py:294
  99.1 0.0 all-to-all-done.1.got_ref
  99.1 0.0 copy-start.1
  99.1 0.8 copy-done.1
  99.9 1.9 %shard_map.71 = f32[128,768]{1,0:T(8,128)} custom-call(f32[4,128,256]{2,1,0:T(8,128)} %copy-done.1), custom_call_target="tpu_custom_call" | custom-call | flops 262144 | bytes 1048576 | tf_op jit(solution)/shard_map/pallas_call | solution.py:307
Async XLA Ops:
  7.1 55.5 %all-to-all-start = ((f32[128,1,6272]{2,1,0:T(1,128)}), f32[128,1,6272]{2,1,0:T(1,128)S(1)}, u32[]{:S(2)}, u32[]{:S(2)}) async-start(f32[128,1,6272]{2,1,0:T(1,128)} %bitcast.7), calls=%async_computation | async-start | bytes 6422528 | tf_op jit(solution)/shard_map/all_to_all | solution.py:272
  20.6 38.7 %collective-permute-start = (f32[128,256]{1,0:T(8,128)}, f32[128,256]{1,0:T(8,128)S(1)}, u32[]{:S(2)}, u32[]{:S(2)}) collective-permute-start(f32[128,256]{1,0:T(8,128)} %get-tuple-element.10), channel_id=1, source_target_pairs={{0,1},{1,2},{2,3},{3,0},{4,5},{5,6},{6,7},{7,4},{8,9},{9,10},{10,1... | collective-permute-start | bytes 393224 | tf_op jit(solution)/shard_map/ppermute | solution.py:281
  22.1 40.5 %collective-permute-start.1 = (f32[128,256]{1,0:T(8,128)}, f32[128,256]{1,0:T(8,128)S(1)}, u32[]{:S(2)}, u32[]{:S(2)}) collective-permute-start(f32[128,256]{1,0:T(8,128)} %get-tuple-element.11), channel_id=1, source_target_pairs={{0,2},{1,3},{2,0},{3,1},{4,6},{5,7},{6,4},{7,5},{8,10},{9,11},{10,... | collective-permute-start | bytes 393224 | tf_op jit(solution)/shard_map/ppermute | solution.py:281
  25.0 37.6 %collective-permute-start.2 = (f32[128,256]{1,0:T(8,128)}, f32[128,256]{1,0:T(8,128)}, u32[]{:S(2)}, u32[]{:S(2)}) collective-permute-start(f32[128,256]{1,0:T(8,128)} %get-tuple-element.12), channel_id=1, source_target_pairs={{0,3},{1,0},{2,1},{3,2},{4,7},{5,4},{6,5},{7,6},{8,11},{9,8},{10,9... | collective-permute-start | bytes 393224 | tf_op jit(solution)/shard_map/ppermute | solution.py:281
  59.3 3.3 %copy-start.2 = (f32[128,256]{1,0:T(8,128)}, f32[128,256]{1,0:T(8,128)S(1)}, u32[]{:S(2)}) copy-start(f32[128,256]{1,0:T(8,128)S(1)} %collective-permute-done.one_ref) | copy-start | bytes 393220
  62.6 0.6 copy-start.3
  62.6 1.7 %copy-start = (f32[128,1,6272]{2,1,0:T(1,128)}, f32[128,1,6272]{2,1,0:T(1,128)S(1)}, u32[]{:S(2)}) copy-start(f32[128,1,6272]{2,1,0:T(1,128)S(1)} %all-to-all-done) | copy-start | bytes 9633796
  69.4 29.7 %all-to-all-start.1 = ((f32[4,128,256]{2,1,0:T(8,128)}), f32[4,128,256]{2,1,0:T(8,128)S(1)}, u32[]{:S(2)}, u32[]{:S(2)}) async-start(f32[4,128,256]{2,1,0:T(8,128)} %get-tuple-element.13.cent_ref), calls=%async_computation.1 | async-start | bytes 1048576 | tf_op jit(solution)/shard_map/all_to_all | solution.py:293
  99.1 0.8 copy-start.1

commit v2 on v1

v2 whole, which is shorter than its diff:
```python
import functools
import jax
import jax.numpy as jnp
from jax import lax
from jax.experimental import pallas as pl
from jax.experimental.pallas import tpu as pltpu
from jax.sharding import PartitionSpec as P

prior_weight = 8.0
F32 = jnp.float32
BF16 = jnp.bfloat16
VMEM = pl.BlockSpec(memory_space=pltpu.VMEM)
SMEM = pl.BlockSpec(memory_space=pltpu.SMEM)
HBM = pl.BlockSpec(memory_space=pltpu.HBM)
DMA = pltpu.SemaphoreType.DMA
LIMIT = 58 * 2**20

ALL = {"owners": (0, 1, 2, 3), "narrow": (((0, 1), 32), ((2, 3), 40)), "labels": 48, "rows": 49}


def split2(x):
    first = x.astype(BF16)
    return first, (x - first.astype(F32)).astype(BF16)


def split3(x):
    first, second = split2(x)
    third = (x - first.astype(F32) - second.astype(F32)).astype(BF16)
    return first, second, third


def iota(shape, dim):
    return lax.broadcasted_iota(jnp.int32, shape, dim)


def dot(a, b):
    return jnp.dot(a, b, preferred_element_type=F32)


def pack_kernel(
    chunk, parts, dest_hbm, label_hbm, rows_hbm, out_hbm, dest_ref, label_ref, rows_ref, out_ref, a_ref, b_ref, sem
):
    owners, message = chunk["owners"], chunk["rows"]
    count = len(owners)
    loads = [
        pltpu.make_async_copy(src, dst, sem.at[i])
        for i, (src, dst) in enumerate(((dest_hbm, dest_ref), (label_hbm, label_ref), (rows_hbm, rows_ref)))
    ]
    for load in loads:
        load.start()
    loads[0].wait()
    dest = dest_ref[...]
    named = (iota((128, 512), 0) == dest).astype(F32)
    earlier = (iota((512, 512), 0) < iota((512, 512), 1)).astype(BF16)
    before = dot(named.astype(BF16), earlier)
    spot = jnp.sum(named * before, axis=0, keepdims=True).astype(jnp.int32)
    shard, owner = dest // 4, dest % 4
    place = (owner - owners[0]) * 8 + spot
    chosen = (owner >= owners[0]) & (owner <= owners[-1])
    slot = jnp.where(chosen, shard * (8 * count) + place, -1)

    loads[1].wait()
    if chunk["labels"] is not None:
        group = (iota((32, 512), 0) == shard).astype(F32)
        within = (iota((128, 512), 0) == owner * 8 + spot).astype(BF16)
        labels = group * (label_ref[...] + 1).astype(F32)
        label_rows = lax.dot_general(
            labels.astype(BF16), within, (((1,), (1,)), ((), ())), preferred_element_type=F32
        ) - 1.0
        for quarter in range(4):
            out_ref[pl.ds(message * quarter + chunk["labels"], 32, stride=4 * message), :] = label_rows

    loads[2].wait()
    low = iota((512, 128), 1) < 64
    tile = [rows_ref[:, 128 * i : 128 * i + 128] for i in range(6)]
    wide = [
        tile[0],
        pltpu.roll(jnp.where(low, tile[2], tile[1]), 64, 1),
        tile[3],
        pltpu.roll(jnp.where(low, tile[5], tile[4]), 64, 1),
    ]
    narrow = [jnp.where(low, tile[1], tile[2]), jnp.where(low, tile[4], tile[5])]
    for i, block in enumerate(wide + narrow):
        for piece, part in enumerate(split2(block)):
            a_ref[512 * piece : 512 * piece + 512, 128 * i : 128 * i + 128] = part

    lower = iota((8, 128), 1) < 64
    stores = []
    groups = 32 // parts
    for part in range(parts):
        size = groups * 8 * count
        pick = (iota((size, 512), 0) + size * part == slot).astype(BF16)
        got = b_ref.at[part % 2]
        got[...] = dot(pick, a_ref[0:512, :]) + dot(pick, a_ref[512:1024, :])
        for s in range(groups):
            for quarter in range(4):
                base = message * (4 * (groups * part + s) + quarter)
                at = 8 * count * s
                out_ref[pl.ds(base, 8 * count), :] = got[at : at + 8 * count, 128 * quarter : 128 * quarter + 128]
                lanes = 512 + 128 * (quarter // 2)
                for members, offset in chunk["narrow"]:
                    rows = [at + 8 * (r - owners[0]) for r in members]
                    one = got[rows[0] : rows[0] + 8, lanes : lanes + 128]
                    if len(members) == 2:
                        two = got[rows[1] : rows[1] + 8, lanes : lanes + 128]
                    else:
                        two = pltpu.roll(one, 4, 0)
                    if quarter % 2 == 0:
                        both = jnp.where(lower, one, pltpu.roll(two, 64, 1))
                    else:
                        both = jnp.where(lower, pltpu.roll(one, 64, 1), two)
                    height = 4 * len(members)
                    out_ref[pl.ds(base + offset, height), :] = both[0:height]
        span = pl.ds(128 * message // parts * part, 128 * message // parts)
        stores.append(pltpu.make_async_copy(out_ref.at[span], out_hbm.at[span], sem.at[3 + part]))
        stores[-1].start()
    for store in stores:
        store.wait()


def fold(block):
    return jnp.where(iota((64, 128), 1) < 64, block[0:64], pltpu.roll(block[64:128], 64, 1))


def unfold(block):
    return jnp.concatenate([block, pltpu.roll(block, 64, 1)], axis=0)


def quarters_kernel(rep_ref, old_ref, own_ref, one_ref, two_ref, three_ref):
    rep = rep_ref[0]
    low = iota((128, 128), 1) < 64
    tile = [old_ref[:, 128 * i : 128 * i + 128] for i in range(6)]
    wide = [
        tile[0],
        pltpu.roll(jnp.where(low, tile[2], tile[1]), 64, 1),
        tile[3],
        pltpu.roll(jnp.where(low, tile[5], tile[4]), 64, 1),
    ]
    narrow = [tile[1], pltpu.roll(tile[2], 64, 1), tile[4], pltpu.roll(tile[5], 64, 1)]
    for step, ref in enumerate((own_ref, one_ref, two_ref, three_ref)):
        which = lax.rem(rep + step, 4)
        for start, choice in ((0, wide), (128, [fold(block) for block in narrow])):
            ref[start : start + choice[0].shape[0], :] = jnp.where(
                which == 0,
                choice[0],
                jnp.where(which == 1, choice[1], jnp.where(which == 2, choice[2], choice[3])),
            )


def book_kernel(book_ref, out_ref):
    for g in range(4):
        words = book_ref[:, 8 * g : 8 * g + 8, :].reshape(48, 256)
        norm = jnp.sum((words * words).reshape(6, 8, 256), axis=0)
        first, second, third = (part.astype(F32) for part in split3(-2.0 * words))
        n1, n2, n3 = (part.astype(F32) for part in split3(norm))
        stack = jnp.concatenate([first, second, third, first, second], axis=0)
        for m in range(8):
            mine = jnp.where(iota((240, 256), 0) % 8 == m, stack, 0.0)
            tail_row = iota((16, 256), 0)
            tail = jnp.where(
                tail_row == 0,
                n1[m : m + 1],
                jnp.where(tail_row == 1, n2[m : m + 1], jnp.where(tail_row == 2, n3[m : m + 1], 0.0)),
            )
            out_ref[8 * g + m] = jnp.concatenate([mine, tail], axis=0).T.astype(BF16)


def centroid_kernel(chunk, rep_ref, got_hbm, own_hbm, one_hbm, two_hbm, three_hbm, *refs):
    owners, message = chunk["owners"], chunk["rows"]
    count = len(owners)
    first = chunk["labels"] is not None
    if first:
        back_hbm, cent_hbm, turned_hbm, lab_hbm = refs[:4]
        refs = refs[4:]
    else:
        lab_hbm, _, back_hbm, cent_hbm, turned_hbm = refs[:5]
        refs = refs[5:]
    got_ref, old_ref, back_ref, cent_ref, lab_ref, turned_ref, flip_ref, sem = refs
    rep = rep_ref[0]
    half = 64 * message
    loads = [
        pltpu.make_async_copy(got_hbm.at[pl.ds(half * i, half)], got_ref.at[pl.ds(half * i, half)], sem.at[4 + i])
        for i in range(2)
    ] + [
        pltpu.make_async_copy(src, old_ref.at[i], sem.at[i])
        for i, src in enumerate((own_hbm, one_hbm, two_hbm, three_hbm))
    ]
    if not first:
        loads.append(pltpu.make_async_copy(lab_hbm, lab_ref, sem.at[6]))
    for load in loads:
        load.start()
    if not first:
        loads[6].wait()
    stores = []

    def store(src, dst, at):
        stores.append(pltpu.make_async_copy(src, dst, sem.at[at]))
        stores[-1].start()

    posting = iota((128, 128), 0).astype(F32)
    early = iota((128, 128), 0) % 8 < 4
    spread = (iota((128, 512), 0) == (iota((128, 512), 1) // 128) * 8 + iota((128, 512), 1) % 8).astype(BF16)
    keep = iota((64, 512), 0) % 16 == (iota((64, 512), 1) % 128) // 8
    sums = [None] * count
    counts = [None] * count
    for part in range(2):
        loads[part].wait()
        if first:
            lab = got_ref[pl.ds(half * part + chunk["labels"], 64, stride=message), :].astype(BF16)
            moved = jnp.where(keep, dot(lab, spread), 0.0)
            lab_rows = jnp.sum(moved.reshape(4, 16, 512), axis=1)
            lab_ref[4 * part : 4 * part + 4, :] = lab_rows
        else:
            lab_rows = lab_ref[4 * part : 4 * part + 4, :]
        for c in range(4 * part, 4 * part + 4):
            senders = range(16 * c, 16 * c + 16)
            for members, offset in chunk["narrow"]:
                if len(members) == 2:
                    narrow = jnp.concatenate([got_ref[pl.ds(message * q + offset, 8), :] for q in senders], axis=0)
                else:
                    block = jnp.concatenate(
                        [got_ref[pl.ds(message * q + offset - 4, 8), :] for q in senders], axis=0
                    )
                    narrow = jnp.where(early, pltpu.roll(block, 124, 0), pltpu.roll(block, 64, 1))
                narrow_parts = split2(narrow)
                narrow_turned = narrow.T
                for k, r in enumerate(members):
                    i = r - owners[0]
                    wide = jnp.concatenate([got_ref[pl.ds(message * q + 8 * i, 8), :] for q in senders], axis=0)
                    labels = lab_rows[c - 4 * part : c - 4 * part + 1, 128 * r : 128 * r + 128]
                    hot = (posting == labels).astype(F32)
                    wide_parts = split2(wide)
                    right = jnp.concatenate(
                        [jnp.concatenate([a, b], axis=1) for a, b in zip(wide_parts, narrow_parts)], axis=0
                    )
                    left = hot.astype(BF16)
                    total = dot(jnp.concatenate([left, left], axis=1), right)
                    sums[i] = total if sums[i] is None else sums[i] + total
                    counts[i] = hot if counts[i] is None else counts[i] + hot
                    turned_ref[c, i, 0:128, :] = wide.T
                    turned_ref[c, i, 128:192, :] = narrow_turned[64 * k : 64 * k + 64]
        span = pl.ds(4 * part, 4)
        store(turned_ref.at[span], turned_hbm.at[span], 7 + part)
    for load in loads[2:6]:
        load.wait()
    for members, _ in chunk["narrow"]:
        for k, r in enumerate(members):
            i = r - owners[0]
            step = lax.rem(rep - r + 4, 4)
            weight = prior_weight + jnp.sum(counts[i], axis=1, keepdims=True)
            old = old_ref[step]
            wide = (prior_weight * old[0:128] + sums[i][:, 0:128]) / weight
            tail = sums[i][:, 128:256]
            if k:
                tail = pltpu.roll(tail, 64, 1)
            narrow = (prior_weight * unfold(old[128:192]) + tail) / weight
            back_ref[i, 0:128, :] = wide
            back_ref[i, 128:192, :] = fold(narrow)
            flip_ref[0:128, :] = wide.T
            flip_ref[128:192, :] = narrow.T[0:64]
            for g in range(4):
                for t in range(6):
                    rows = flip_ref[pl.ds(48 * g + t, 8, stride=6), :]
                    for piece, block in enumerate(split2(rows)):
                        at = 48 * piece + 8 * t
                        cent_ref[4 * i + g, at : at + 8, :] = block.astype(F32)
    store(cent_ref, cent_hbm, 9)
    store(back_ref, back_hbm.at[pl.ds(owners[0], count)], 10)
    if first:
        store(lab_ref, lab_hbm, 11)
    for copy in stores:
        copy.wait()


def score_kernel(chunk, turned_hbm, cent_hbm, lab_hbm, book_hbm, *refs):
    if chunk["labels"] is None:
        refs = refs[1:]
    out_hbm, turned_ref, cent2_ref, lab_ref, book_ref, res_ref, norm_ref, out_ref, sem = refs
    owners = chunk["owners"]
    count = len(owners)

    def fetch(src, dst, at):
        return pltpu.make_async_copy(src, dst, sem.at[at])

    def fetch_turned(r):
        return fetch(turned_hbm.at[:, r], turned_ref.at[:, r], r)

    def fetch_book(g):
        return fetch(book_hbm.at[pl.ds(8 * g, 8)], book_ref.at[pl.ds(8 * g, 8)], 4 + g)

    small = [fetch(lab_hbm, lab_ref, 8), fetch(cent_hbm, cent2_ref, 9)]
    for copy in small:
        copy.start()
    fetch_turned(0).start()
    for g in range(4):
        fetch_book(g).start()
    for r in range(1, count):
        fetch_turned(r).start()
    ones = jnp.where(iota((16, 1024), 0) < 3, 1.0, 0.0).astype(BF16)
    res_ref[0, 240:256, :] = ones
    res_ref[1, 240:256, :] = ones
    for copy in small:
        copy.wait()
    fetch_turned(0).wait()

    def prepare(i, buffer):
        r = i // 4
        g = i % 4
        labs = lab_ref[:, pl.ds(pl.multiple_of(128 * (r + owners[0]), 128), 128)]
        posting = iota((128, 128), 0).astype(F32)
        hot = jnp.concatenate([(posting == labs[c : c + 1]).astype(BF16) for c in range(8)], axis=1)
        part = dot(cent2_ref[i].astype(BF16), hot)
        near = part[0:48] + part[48:96]
        rows = jnp.concatenate(
            [
                jnp.concatenate([turned_ref[c, r, pl.ds(48 * g + t, 8, stride=6), :] for c in range(8)], axis=1)
                for t in range(6)
            ],
            axis=0,
        )
        res = rows - near
        norm_ref[buffer] = jnp.sum((res * res).reshape(6, 8, 1024), axis=0)
        first, second = split2(res)
        for spot, piece in enumerate((first, first, first, second, second)):
            res_ref[buffer, 48 * spot : 48 * spot + 48, :] = piece

    def score(i, buffer):
        r = i // 4
        g = i % 4
        right = res_ref[buffer]
        best = []
        for m in range(8):
            value = dot(book_ref[8 * g + m], right)
            value = jnp.min(value.reshape(32, 8, 1024), axis=0)
            best.append(jnp.min(value, axis=0, keepdims=True))
        out_ref[pl.ds(pl.multiple_of(8 * g, 8), 8), pl.ds(pl.multiple_of(1024 * r, 1024), 1024)] = (
            jnp.concatenate(best, axis=0) + norm_ref[buffer]
        )

    prepare(0, 0)

    def step(k, carry):
        @pl.when(k < 4 // 2)
        def _():
            for u in range(2):
                fetch_book(k * 2 + u).wait()

        @pl.when((k % (4 // 2) == 4 // 2 - 1) & (k < 4 * count // 2 - 1))
        def _():
            fetch_turned((k + 1) * 2 // 4).wait()

        for u in range(2):
            i = k * 2 + u
            score(i, u % 2 if 2 > 1 else i % 2)
            prepare(jnp.minimum(i + 1, 4 * count - 1), (u + 1) % 2 if 2 > 1 else (i + 1) % 2)
        return carry

    lax.fori_loop(0, 4 * count // 2, step, 0)
    done = fetch(out_ref, out_hbm.at[:, pl.ds(1024 * owners[0], 1024 * count)], 10)
    done.start()
    done.wait()


def join_kernel(got_ref, out_ref):
    low = iota((128, 128), 1) < 64
    for half in range(2):
        wide0, narrow0 = got_ref[2 * half, 0:128, :], unfold(got_ref[2 * half, 128:192, :])
        wide1, narrow1 = got_ref[2 * half + 1, 0:128, :], unfold(got_ref[2 * half + 1, 128:192, :])
        turned = pltpu.roll(wide1, 64, 1)
        at = 384 * half
        out_ref[:, at : at + 128] = wide0
        out_ref[:, at + 128 : at + 256] = jnp.where(low, narrow0, turned)
        out_ref[:, at + 256 : at + 384] = jnp.where(low, turned, pltpu.roll(narrow1, 64, 1))


def call(kernel, out_shape, specs, out_specs, scratch=(), flops=0, moved=0, limit=LIMIT, aliases=None):
    return pl.pallas_call(
        kernel,
        out_shape=out_shape,
        in_specs=specs,
        out_specs=out_specs,
        scratch_shapes=scratch,
        input_output_aliases=aliases or {},
        compiler_params=pltpu.CompilerParams(vmem_limit_bytes=limit),
        cost_estimate=pl.CostEstimate(flops=flops, bytes_accessed=moved, transcendentals=0),
    )


def shape(*dims, dtype=F32):
    return jax.ShapeDtypeStruct(dims, dtype)


def pack_call(chunk, parts, destination, labels, embeddings):
    message, count = chunk["rows"], len(chunk["owners"])
    return call(
        functools.partial(pack_kernel, chunk, parts),
        shape(128 * message, 128),
        [HBM] * 3,
        HBM,
        [
            pltpu.VMEM((1, 512), jnp.int32),
            pltpu.VMEM((1, 512), jnp.int32),
            pltpu.VMEM((512, 768), F32),
            pltpu.VMEM((128 * message, 128), F32),
            pltpu.VMEM((1024, 768), BF16),
            pltpu.VMEM((2, 256 * count // parts, 768), F32),
            DMA((3 + parts,)),
        ],
        flops=2 * 256 * count * 512 * 768 * 2,
        moved=5 * 2**20,
    )(destination, labels, embeddings)


def exchange(chunk, outgoing):
    message = chunk["rows"]
    return lax.all_to_all(
        outgoing.reshape(128, 1, message * 128), ("shard", "rep"), split_axis=0, concat_axis=0, tiled=True
    ).reshape(128 * message, 128)


def centroid_call(chunk, rep, received, olds, rest):
    message, count = chunk["rows"], len(chunk["owners"])
    first = chunk["labels"] is not None
    outs = [shape(4, 192, 128), shape(4 * count, 96, 128), shape(8, count, 192, 128)]
    if first:
        outs.append(shape(8, 512))
    return call(
        functools.partial(centroid_kernel, chunk),
        outs,
        [SMEM] + [HBM] * (5 + len(rest)),
        [HBM] * len(outs),
        [
            pltpu.VMEM((128 * message, 128), F32),
            pltpu.VMEM((4, 192, 128), F32),
            pltpu.VMEM((count, 192, 128), F32),
            pltpu.VMEM((4 * count, 96, 128), F32),
            pltpu.VMEM((8, 512), F32),
            pltpu.VMEM((8, count, 192, 128), F32),
            pltpu.VMEM((192, 128), F32),
            DMA((12,)),
        ],
        flops=2**28,
        moved=2**23,
        aliases={} if first else {7: 0},
    )(rep, received, *olds, *rest)


def score_call(chunk, turned, cents, lab_rows, book, rest):
    count = len(chunk["owners"])
    return call(
        functools.partial(score_kernel, chunk),
        shape(32, 4096),
        [HBM] * (4 + len(rest)),
        HBM,
        [
            pltpu.VMEM((8, count, 192, 128), F32),
            pltpu.VMEM((4 * count, 96, 128), F32),
            pltpu.VMEM((8, 512), F32),
            pltpu.VMEM((32, 256, 256), BF16),
            pltpu.VMEM((2, 256, 1024), BF16),
            pltpu.VMEM((2, 8, 1024), F32),
            pltpu.VMEM((32, 1024 * count), F32),
            DMA((11,)),
        ],
        flops=2**28,
        moved=2**23,
        aliases={4: 0} if rest else {},
    )(turned, cents, lab_rows, book, *rest)


def local(embeddings, destination, labels, old_centroids, codebook):
    rep = lax.axis_index("rep").astype(jnp.int32).reshape(1)
    destination, labels = destination.reshape(1, 512), labels.reshape(1, 512)
    outgoing = pack_call(ALL, 4, destination, labels, embeddings)
    quarters = call(
        quarters_kernel, [shape(192, 128)] * 4, [SMEM, VMEM], [VMEM] * 4, flops=2**20, moved=2**20
    )(rep, old_centroids)
    olds = [quarters[0]]
    for step in (1, 2, 3):
        olds.append(lax.ppermute(quarters[step], "rep", [(i, (i + step) % 4) for i in range(4)]))
    book = call(
        book_kernel, shape(32, 256, 256, dtype=BF16), [VMEM], VMEM, flops=2**28, moved=5 * 2**20
    )(jnp.transpose(codebook, (2, 0, 1)))

    received = exchange(ALL, outgoing)
    received, book = lax.optimization_barrier((received, book))
    back, cents, turned, lab_rows = centroid_call(ALL, rep, received, olds, ())
    returned = lax.all_to_all(back, "rep", split_axis=0, concat_axis=0, tiled=True)
    scores = score_call(ALL, turned, cents, lab_rows, book, ())
    centroids = call(join_kernel, shape(128, 768), [VMEM], VMEM, flops=2**18, moved=2**20, limit=16 * 2**20)(returned)
    return (centroids, scores)


def solution(mesh):
    placed = (
        P(("shard", "rep"), None),
        P(("shard", "rep"), None),
        P(("shard", "rep")),
        P(("shard", "rep"), None),
        P("rep", None, None),
    )
    return jax.shard_map(
        local,
        mesh=mesh,
        in_specs=placed,
        out_specs=(P(("shard", "rep"), None), P("rep", "shard")),
        check_vma=False,
    )
```

time: 102 us -> 94.2 us (0.924)
  Pallas kernels: 45.8 us -> 39.8 us
  waiting for transfers between devices: 32.5 us -> 31.3 us
    ppermute x3, waiting for transfers between devices: 32.5 us -> 0.01 us  [local(): lax.ppermute(quarters[step], 'rep', [(i, (i + step) % 4) for i in range(4)])]
    all_to_all x2, waiting for transfers between devices: 0.01 us -> 31.3 us  [the longest x1 31.3 us: exchange(): lax.all_to_all(outgoing.reshape(128, 1, message * 128), ('shard', 'rep'),...]
    pallas_call x6, Pallas kernels: 45.8 us -> 39.8 us  [the longest x1 23.9 us: score_call(): call(functools.partial(score_kernel, chunk), shape(32, 4096), [HBM] * (4...]
  transfers between devices with their start and end apart: 5 -> 5, of which waited for: 2 -> 1; matrix products, arithmetic and copies ran while one was open for 0% -> 0% of each run, Pallas kernels for 32% -> 32%
where the time goes in v2:
time: 94.2 us; the launch traced here: 93.9 us
  Pallas kernels  39.8 us (42%)
  waiting for transfers between devices  31.3 us (33%)
  starting transfers between devices  20.3 us (22%)
  local copies, waits for them, and re-layouts  1.74 us (2%)
    all_to_all x1, waiting for transfers between devices, exchange(): lax.all_to_all(outgoing.reshape(128, 1, message * 128), ('shard', 'rep'),...  31.3 us
    pallas_call x1, Pallas kernels, score_call(): call(functools.partial(score_kernel, chunk), shape(32, 4096), [HBM] * (4...  23.9 us
    all_to_all x1, starting transfers between devices, exchange(): lax.all_to_all(outgoing.reshape(128, 1, message * 128), ('shard', 'rep'),...  11.5 us
    ppermute x3, starting transfers between devices, local(): lax.ppermute(quarters[step], 'rep', [(i, (i + step) % 4) for i in range(4)])  5.35 us
    pallas_call x1, Pallas kernels, pack_call(): call(functools.partial(pack_kernel, chunk, parts), shape(128 * message, 1...  4.5 us
    pallas_call x1, Pallas kernels, centroid_call(): call(functools.partial(centroid_kernel, chunk), outs, [SMEM] + [HBM] * (5...  4.36 us
    pallas_call x1, Pallas kernels, local(): call(book_kernel, shape(32, 256, 256, dtype=BF16), [VMEM], VMEM, flops=2...  4.15 us
    all_to_all x1, starting transfers between devices, local(): lax.all_to_all(back, 'rep', split_axis=0, concat_axis=0, tiled=True)  3.47 us
  transfers between devices with their start and end apart: 5, of which 1 were waited for; matrix products, arithmetic and copies ran while one was open for 0% of the time, Pallas kernels for 32%

profile of v2, /device:TPU:1, one launch (start us, length us, event | category | flops | bytes accessed | tf_op | source)
XLA Modules:
  0.0 93.9 jit_solution(9470262039430244366)
XLA Ops:
  0.6 4.5 %shard_map.68 = f32[6272,128]{1,0:T(8,128)} custom-call(s32[1,512]{1,0:T(1,128)} %bitcast.9, s32[1,512]{1,0:T(1,128)} %bitcast.10, f32[512,768]{1,0:T(8,128)} %rows_hbm.1), custom_call_target="tpu_custom_call" | custom-call | flops 1610612736 | bytes 5242880 | tf_op jit(solution)/shard_map/pallas_call | solution.py:395
  5.1 11.5 %all-to-all-start = ((f32[128,1,6272]{2,1,0:T(1,128)}), f32[128,1,6272]{2,1,0:T(1,128)S(1)}, u32[]{:S(2)}, u32[]{:S(2)}) async-start(f32[128,1,6272]{2,1,0:T(1,128)} %bitcast.7), calls=%async_computation | async-start | bytes 6422528 | tf_op jit(solution)/shard_map/all_to_all | solution.py:416
  16.7 1.9 %shard_map.70 = (f32[192,128]{1,0:T(8,128)}, f32[192,128]{1,0:T(8,128)}, f32[192,128]{1,0:T(8,128)}, f32[192,128]{1,0:T(8,128)}) custom-call(s32[1]{0:T(128)} %bitcast.rep_ref, f32[128,768]{1,0:T(8,128)} %old_ref.1), custom_call_target="tpu_custom_call" | custom-call | flops 1048576 | bytes 1048576 | tf_op jit(solution)/shard_map/pallas_call | solution.py:475
  18.6 1.5 %collective-permute-start = (f32[192,128]{1,0:T(8,128)}, f32[192,128]{1,0:T(8,128)S(1)}, u32[]{:S(2)}, u32[]{:S(2)}) collective-permute-start(f32[192,128]{1,0:T(8,128)} %get-tuple-element.14), channel_id=1, source_target_pairs={{0,1},{1,2},{2,3},{3,0},{4,5},{5,6},{6,7},{7,4},{8,9},{9,10},{10,1... | collective-permute-start | bytes 294920 | tf_op jit(solution)/shard_map/ppermute | solution.py:480
  20.1 2.9 %collective-permute-start.1 = (f32[192,128]{1,0:T(8,128)}, f32[192,128]{1,0:T(8,128)S(1)}, u32[]{:S(2)}, u32[]{:S(2)}) collective-permute-start(f32[192,128]{1,0:T(8,128)} %get-tuple-element.15), channel_id=1, source_target_pairs={{0,2},{1,3},{2,0},{3,1},{4,6},{5,7},{6,4},{7,5},{8,10},{9,11},{10,... | collective-permute-start | bytes 294920 | tf_op jit(solution)/shard_map/ppermute | solution.py:480
  23.0 0.9 collective-permute-start.2
  23.9 4.1 %shard_map.69.book_hbm = bf16[32,256,256]{2,1,0:T(8,128)(2,1)} custom-call(f32[6,32,256]{2,1,0:T(8,128)} %bitcast.8), custom_call_target="tpu_custom_call" | custom-call | flops 268435456 | bytes 5242880 | tf_op jit(solution)/shard_map/pallas_call | solution.py:481
  28.1 31.3 %all-to-all-done = f32[128,1,6272]{2,1,0:T(1,128)S(1)} async-done(((f32[128,1,6272]{2,1,0:T(1,128)}), f32[128,1,6272]{2,1,0:T(1,128)S(1)}, u32[]{:S(2)}, u32[]{:S(2)}) %all-to-all-start) | async-done | bytes 3211296 | tf_op jit(solution)/shard_map/all_to_all | solution.py:416
  59.4 0.0 copy-start
  59.4 0.0 collective-permute-done.one_hbm
  59.4 0.0 copy-start.1
  59.4 0.0 collective-permute-done.1.two_hbm
  59.4 0.0 copy-start.2
  59.4 0.0 collective-permute-done.2.three_hbm
  59.4 0.0 copy-start.3
  59.5 1.7 %copy-done = f32[128,1,6272]{2,1,0:T(1,128)} copy-done((f32[128,1,6272]{2,1,0:T(1,128)}, f32[128,1,6272]{2,1,0:T(1,128)S(1)}, u32[]{:S(2)}) %copy-start) | copy-done | bytes 3211288
  61.1 0.0 copy-done.1
  61.1 0.0 copy-done.2
  61.2 0.0 copy-done.3
  61.2 4.4 %shard_map.71 = (f32[4,192,128]{2,1,0:T(8,128)}, f32[16,96,128]{2,1,0:T(8,128)}, f32[8,4,192,128]{3,2,1,0:T(8,128)}, f32[8,512]{1,0:T(8,128)}) custom-call(s32[1]{0:T(128)} %bitcast.rep_ref, f32[6272,128]{1,0:T(8,128)} %bitcast.6, f32[192,128]{1,0:T(8,128)} %get-tuple-element.13.own_hbm, f32[192,128]{1,0:T(8,128)} %copy-done.1, f32[192,128]{1,0:T(8,128)} %copy-done.2, ...), custom_call_target="tpu_custom_call" | custom-call | flops 268435456 | bytes 8388608 | tf_op jit(solution)/shard_map/pallas_call | solution.py:427
  65.6 3.5 %all-to-all-start.1 = ((f32[4,192,128]{2,1,0:T(8,128)}), f32[4,192,128]{2,1,0:T(8,128)S(1)}, u32[]{:S(2)}, u32[]{:S(2)}) async-start(f32[4,192,128]{2,1,0:T(8,128)} %get-tuple-element.17), calls=%async_computation.1 | async-start | bytes 786432 | tf_op jit(solution)/shard_map/all_to_all | solution.py:488
  69.0 23.9 %shard_map.73 = f32[32,4096]{1,0:T(8,128)} custom-call(f32[8,4,192,128]{3,2,1,0:T(8,128)} %get-tuple-element.18.turned_hbm, f32[16,96,128]{2,1,0:T(8,128)} %get-tuple-element.19.cent_hbm, f32[8,512]{1,0:T(8,128)} %get-tuple-element.20.lab_hbm, bf16[32,256,256]{2,1,0:T(8,128)(2,1)} %shard_map.69.book_hbm), custom_call_target="tpu_custom_call" | custom-call | flops 268435456 | bytes 8388608 | tf_op jit(solution)/shard_map/pallas_call | solution.py:450
  93.0 0.0 all-to-all-done.1.got_ref
  93.0 0.9 shard_map.72
Async XLA Ops:
  5.1 54.3 %all-to-all-start = ((f32[128,1,6272]{2,1,0:T(1,128)}), f32[128,1,6272]{2,1,0:T(1,128)S(1)}, u32[]{:S(2)}, u32[]{:S(2)}) async-start(f32[128,1,6272]{2,1,0:T(1,128)} %bitcast.7), calls=%async_computation | async-start | bytes 6422528 | tf_op jit(solution)/shard_map/all_to_all | solution.py:416
  18.6 40.8 %collective-permute-start = (f32[192,128]{1,0:T(8,128)}, f32[192,128]{1,0:T(8,128)S(1)}, u32[]{:S(2)}, u32[]{:S(2)}) collective-permute-start(f32[192,128]{1,0:T(8,128)} %get-tuple-element.14), channel_id=1, source_target_pairs={{0,1},{1,2},{2,3},{3,0},{4,5},{5,6},{6,7},{7,4},{8,9},{9,10},{10,1... | collective-permute-start | bytes 294920 | tf_op jit(solution)/shard_map/ppermute | solution.py:480
  20.1 39.3 %collective-permute-start.1 = (f32[192,128]{1,0:T(8,128)}, f32[192,128]{1,0:T(8,128)S(1)}, u32[]{:S(2)}, u32[]{:S(2)}) collective-permute-start(f32[192,128]{1,0:T(8,128)} %get-tuple-element.15), channel_id=1, source_target_pairs={{0,2},{1,3},{2,0},{3,1},{4,6},{5,7},{6,4},{7,5},{8,10},{9,11},{10,... | collective-permute-start | bytes 294920 | tf_op jit(solution)/shard_map/ppermute | solution.py:480
  23.0 36.4 %collective-permute-start.2 = (f32[192,128]{1,0:T(8,128)}, f32[192,128]{1,0:T(8,128)S(1)}, u32[]{:S(2)}, u32[]{:S(2)}) collective-permute-start(f32[192,128]{1,0:T(8,128)} %get-tuple-element.16), channel_id=1, source_target_pairs={{0,3},{1,0},{2,1},{3,2},{4,7},{5,4},{6,5},{7,6},{8,11},{9,8},{10,9... | collective-permute-start | bytes 294920 | tf_op jit(solution)/shard_map/ppermute | solution.py:480
  59.4 1.7 %copy-start = (f32[128,1,6272]{2,1,0:T(1,128)}, f32[128,1,6272]{2,1,0:T(1,128)S(1)}, u32[]{:S(2)}) copy-start(f32[128,1,6272]{2,1,0:T(1,128)S(1)} %all-to-all-done) | copy-start | bytes 9633796
  59.4 1.7 %copy-start.1 = (f32[192,128]{1,0:T(8,128)}, f32[192,128]{1,0:T(8,128)S(1)}, u32[]{:S(2)}) copy-start(f32[192,128]{1,0:T(8,128)S(1)} %collective-permute-done.one_hbm) | copy-start | bytes 294916
  59.4 1.7 %copy-start.2 = (f32[192,128]{1,0:T(8,128)}, f32[192,128]{1,0:T(8,128)S(1)}, u32[]{:S(2)}) copy-start(f32[192,128]{1,0:T(8,128)S(1)} %collective-permute-done.1.two_hbm) | copy-start | bytes 294916
  59.4 1.7 %copy-start.3 = (f32[192,128]{1,0:T(8,128)}, f32[192,128]{1,0:T(8,128)S(1)}, u32[]{:S(2)}) copy-start(f32[192,128]{1,0:T(8,128)S(1)} %collective-permute-done.2.three_hbm) | copy-start | bytes 294916
  65.6 27.4 %all-to-all-start.1 = ((f32[4,192,128]{2,1,0:T(8,128)}), f32[4,192,128]{2,1,0:T(8,128)S(1)}, u32[]{:S(2)}, u32[]{:S(2)}) async-start(f32[4,192,128]{2,1,0:T(8,128)} %get-tuple-element.17), calls=%async_computation.1 | async-start | bytes 786432 | tf_op jit(solution)/shard_map/all_to_all | solution.py:488

commit v3 on v2

v3 whole, which is shorter than its diff:
```python
import functools
import jax
import jax.numpy as jnp
from jax import lax
from jax.experimental import pallas as pl
from jax.experimental.pallas import tpu as pltpu
from jax.sharding import PartitionSpec as P

prior_weight = 8.0
F32 = jnp.float32
BF16 = jnp.bfloat16
VMEM = pl.BlockSpec(memory_space=pltpu.VMEM)
SMEM = pl.BlockSpec(memory_space=pltpu.SMEM)
HBM = pl.BlockSpec(memory_space=pltpu.HBM)
DMA = pltpu.SemaphoreType.DMA
LIMIT = 58 * 2**20
SUMS_LIMIT = 24 * 2**20

ALL = {"owners": (0, 1, 2, 3), "narrow": (((0, 1), 33), ((2, 3), 41)), "labels": 0, "wide": 1, "rows": 49}


def split2(x):
    first = x.astype(BF16)
    return first, (x - first.astype(F32)).astype(BF16)


def split3(x):
    first, second = split2(x)
    third = (x - first.astype(F32) - second.astype(F32)).astype(BF16)
    return first, second, third


def iota(shape, dim):
    return lax.broadcasted_iota(jnp.int32, shape, dim)


def dot(a, b):
    return jnp.dot(a, b, preferred_element_type=F32)


def pack_kernel(
    chunk, parts, dest_hbm, label_hbm, rows_hbm, out_hbm, dest_ref, label_ref, rows_ref, out_ref, a_ref, b_ref, sem
):
    owners, message = chunk["owners"], chunk["rows"]
    count = len(owners)
    loads = [
        pltpu.make_async_copy(src, dst, sem.at[i])
        for i, (src, dst) in enumerate(((dest_hbm, dest_ref), (label_hbm, label_ref), (rows_hbm, rows_ref)))
    ]
    for load in loads:
        load.start()
    loads[0].wait()
    dest = dest_ref[...]
    named = (iota((128, 512), 0) == dest).astype(F32)
    earlier = (iota((512, 512), 0) < iota((512, 512), 1)).astype(BF16)
    before = dot(named.astype(BF16), earlier)
    spot = jnp.sum(named * before, axis=0, keepdims=True).astype(jnp.int32)
    shard, owner = dest // 4, dest % 4
    place = (owner - owners[0]) * 8 + spot
    chosen = (owner >= owners[0]) & (owner <= owners[-1])
    slot = jnp.where(chosen, shard * (8 * count) + place, -1)

    loads[1].wait()
    if chunk["labels"] is not None:
        group = (iota((32, 512), 0) == shard).astype(F32)
        within = (iota((128, 512), 0) == owner * 8 + spot).astype(BF16)
        labels = group * (label_ref[...] + 1).astype(F32)
        label_rows = lax.dot_general(
            labels.astype(BF16), within, (((1,), (1,)), ((), ())), preferred_element_type=F32
        ) - 1.0
        for quarter in range(4):
            out_ref[pl.ds(message * quarter + chunk["labels"], 32, stride=4 * message), :] = label_rows

    loads[2].wait()
    low = iota((512, 128), 1) < 64
    tile = [rows_ref[:, 128 * i : 128 * i + 128] for i in range(6)]
    wide = [
        tile[0],
        pltpu.roll(jnp.where(low, tile[2], tile[1]), 64, 1),
        tile[3],
        pltpu.roll(jnp.where(low, tile[5], tile[4]), 64, 1),
    ]
    narrow = [jnp.where(low, tile[1], tile[2]), jnp.where(low, tile[4], tile[5])]
    for i, block in enumerate(wide + narrow):
        for piece, part in enumerate(split2(block)):
            a_ref[512 * piece : 512 * piece + 512, 128 * i : 128 * i + 128] = part

    lower = iota((8, 128), 1) < 64
    stores = []
    groups = 32 // parts
    for part in range(parts):
        size = groups * 8 * count
        pick = (iota((size, 512), 0) + size * part == slot).astype(BF16)
        got = b_ref.at[part % 2]
        got[...] = dot(pick, a_ref[0:512, :]) + dot(pick, a_ref[512:1024, :])
        for s in range(groups):
            for quarter in range(4):
                base = message * (4 * (groups * part + s) + quarter)
                at = 8 * count * s
                out_ref[pl.ds(base + chunk["wide"], 8 * count), :] = got[at : at + 8 * count, 128 * quarter : 128 * quarter + 128]
                lanes = 512 + 128 * (quarter // 2)
                for members, offset in chunk["narrow"]:
                    rows = [at + 8 * (r - owners[0]) for r in members]
                    one = got[rows[0] : rows[0] + 8, lanes : lanes + 128]
                    two = got[rows[1] : rows[1] + 8, lanes : lanes + 128]
                    if quarter % 2 == 0:
                        both = jnp.where(lower, one, pltpu.roll(two, 64, 1))
                    else:
                        both = jnp.where(lower, pltpu.roll(one, 64, 1), two)
                    out_ref[pl.ds(base + offset, 8), :] = both
        span = pl.ds(128 * message // parts * part, 128 * message // parts)
        stores.append(pltpu.make_async_copy(out_ref.at[span], out_hbm.at[span], sem.at[3 + part]))
        stores[-1].start()
    for store in stores:
        store.wait()


def fold(block):
    return jnp.where(iota((64, 128), 1) < 64, block[0:64], pltpu.roll(block[64:128], 64, 1))


def unfold(block):
    return jnp.concatenate([block, pltpu.roll(block, 64, 1)], axis=0)


def quarters_kernel(rep_ref, old_ref, own_ref, one_ref, two_ref, three_ref):
    rep = rep_ref[0]
    low = iota((128, 128), 1) < 64
    tile = [old_ref[:, 128 * i : 128 * i + 128] for i in range(6)]
    wide = [
        tile[0],
        pltpu.roll(jnp.where(low, tile[2], tile[1]), 64, 1),
        tile[3],
        pltpu.roll(jnp.where(low, tile[5], tile[4]), 64, 1),
    ]
    narrow = [tile[1], pltpu.roll(tile[2], 64, 1), tile[4], pltpu.roll(tile[5], 64, 1)]
    for step, ref in enumerate((own_ref, one_ref, two_ref, three_ref)):
        which = lax.rem(rep + step, 4)
        for start, choice in ((0, wide), (128, [fold(block) for block in narrow])):
            ref[start : start + choice[0].shape[0], :] = jnp.where(
                which == 0,
                choice[0],
                jnp.where(which == 1, choice[1], jnp.where(which == 2, choice[2], choice[3])),
            )


def book_kernel(book_ref, out_ref):
    for g in range(4):
        words = book_ref[:, 8 * g : 8 * g + 8, :].reshape(48, 256)
        norm = jnp.sum((words * words).reshape(6, 8, 256), axis=0)
        first, second, third = (part.astype(F32) for part in split3(-2.0 * words))
        n1, n2, n3 = (part.astype(F32) for part in split3(norm))
        stack = jnp.concatenate([first, second, third, first, second], axis=0)
        for m in range(8):
            mine = jnp.where(iota((240, 256), 0) % 8 == m, stack, 0.0)
            tail_row = iota((16, 256), 0)
            tail = jnp.where(
                tail_row == 0,
                n1[m : m + 1],
                jnp.where(tail_row == 1, n2[m : m + 1], jnp.where(tail_row == 2, n3[m : m + 1], 0.0)),
            )
            out_ref[8 * g + m] = jnp.concatenate([mine, tail], axis=0).T.astype(BF16)


def label_rows(got_ref):
    spread = (iota((128, 512), 0) == (iota((128, 512), 1) // 128) * 8 + iota((128, 512), 1) % 8).astype(BF16)
    keep = iota((128, 512), 0) % 16 == (iota((128, 512), 1) % 128) // 8
    lab = got_ref[pl.ds(ALL["labels"], 128, stride=ALL["rows"]), :].astype(BF16)
    return jnp.sum(jnp.where(keep, dot(lab, spread), 0.0).reshape(8, 16, 512), axis=1)


def tile_rows(got_ref, c, offset):
    return jnp.concatenate([got_ref[pl.ds(ALL["rows"] * q + offset, 8), :] for q in range(16 * c, 16 * c + 16)], axis=0)


def sums_kernel(got_ref, sums_ref):
    posting = iota((128, 128), 0).astype(F32)
    lab = label_rows(got_ref)
    sums = [None] * 4
    counts = [None] * 4
    for c in range(8):
        for members, offset in ALL["narrow"]:
            narrow_parts = split2(tile_rows(got_ref, c, offset))
            for r in members:
                hot = (posting == lab[c : c + 1, 128 * r : 128 * r + 128]).astype(F32)
                right = jnp.concatenate(
                    [
                        jnp.concatenate([a, b], axis=1)
                        for a, b in zip(split2(tile_rows(got_ref, c, ALL["wide"] + 8 * r)), narrow_parts)
                    ],
                    axis=0,
                )
                left = hot.astype(BF16)
                total = dot(jnp.concatenate([left, left], axis=1), right)
                sums[r] = total if sums[r] is None else sums[r] + total
                counts[r] = hot if counts[r] is None else counts[r] + hot
    for members, _ in ALL["narrow"]:
        for k, r in enumerate(members):
            tail = sums[r][:, 128:256]
            if k:
                tail = pltpu.roll(tail, 64, 1)
            sums_ref[r, 0:128, :] = sums[r][:, 0:128]
            sums_ref[r, 128:192, :] = fold(tail)
            sums_ref[r, 192:200, :] = jnp.broadcast_to(jnp.sum(counts[r].T, axis=0, keepdims=True), (8, 128))


def score_kernel(
    rep_ref, got_hbm, sums_hbm, book_hbm, own_hbm, one_hbm, two_hbm, three_hbm, out_hbm,
    got_ref, work_ref, lab_ref, sums_ref, book_ref, old_ref, flip_ref, cent_ref, piece_ref, norm_ref, out_ref, sem,
):
    def fetch(src, dst, at):
        return pltpu.make_async_copy(src, dst, sem.at[at])

    def fetch_book(g):
        return fetch(book_hbm.at[pl.ds(8 * g, 8)], book_ref.at[pl.ds(8 * g, 8)], 4 + g)

    def send(r):
        span = pl.ds(pl.multiple_of(1024 * r, 1024), 1024)
        return fetch(out_ref.at[r], out_hbm.at[:, span], 14 + r)

    rows = []
    for i in range(4):
        span = pl.ds(32 * ALL["rows"] * i, 32 * ALL["rows"])
        rows.append(fetch(got_hbm.at[span], got_ref.at[span], 18 + i))
        rows[i].start()
    small = [fetch(sums_hbm, sums_ref, 8)]
    small += [fetch(src, old_ref.at[i], 10 + i) for i, src in enumerate((own_hbm, one_hbm, two_hbm, three_hbm))]
    for copy in small:
        copy.start()
    for g in range(4):
        fetch_book(g).start()
    rep = rep_ref[0]
    for c in range(8):
        if c % 2 == 0:
            rows[c // 2].wait()
        for members, offset in ALL["narrow"]:
            narrow = tile_rows(got_ref, c, offset).T
            for k, r in enumerate(members):
                at = 192 * (8 * r + c)
                work_ref[at : at + 128, :] = tile_rows(got_ref, c, ALL["wide"] + 8 * r).T
                work_ref[at + 128 : at + 192, :] = narrow[64 * k : 64 * k + 64]
    lab = label_rows(got_ref)
    for copy in small:
        copy.wait()
    for r in range(4):
        lab_ref[r] = lab[:, 128 * r : 128 * r + 128]
        total = prior_weight * old_ref[lax.rem(rep - r + 4, 4)] + sums_ref[r, 0:192, :]
        weight = prior_weight + sums_ref[r, 192:193, :]
        flip_ref[0:128, :] = total[0:128].T / weight
        flip_ref[128:192, :] = unfold(total[128:192]).T[0:64] / weight
        for g in range(4):
            for t in range(6):
                for piece, block in enumerate(split2(flip_ref[pl.ds(48 * g + t, 8, stride=6), :])):
                    at = 192 * piece + 48 * g + 8 * t
                    cent_ref[r, at : at + 8, :] = block.astype(F32)

    def prepare(r, buffer):
        labs = lab_ref[r]
        posting = iota((128, 128), 0).astype(F32)
        hot = jnp.concatenate([(posting == labs[c : c + 1]).astype(BF16) for c in range(8)], axis=1)
        near = dot(cent_ref[r].astype(BF16), hot)
        for g in range(4):
            span = slice(48 * g, 48 * g + 48)
            rows = jnp.concatenate(
                [
                    jnp.concatenate(
                        [work_ref[pl.ds(192 * (8 * r + c) + 48 * g + t, 8, stride=6), :] for c in range(8)], axis=1
                    )
                    for t in range(6)
                ],
                axis=0,
            )
            res = rows - (near[span] + near[192 + 48 * g : 240 + 48 * g])
            norm_ref[buffer, 8 * g : 8 * g + 8, :] = jnp.sum((res * res).reshape(6, 8, 1024), axis=0)
            for i, piece in enumerate(split2(res)):
                piece_ref[buffer, i, span, :] = piece

    ones = jnp.where(iota((16, 1024), 0) < 3, 1.0, 0.0).astype(BF16)

    def score(r, g, buffer):
        first = piece_ref[buffer, 0, 48 * g : 48 * g + 48, :]
        second = piece_ref[buffer, 1, 48 * g : 48 * g + 48, :]
        right = jnp.concatenate([first, first, first, second, second, ones], axis=0)
        best = []
        for m in range(8):
            value = dot(book_ref[8 * g + m], right)
            value = jnp.min(value.reshape(32, 8, 1024), axis=0)
            best.append(jnp.min(value, axis=0, keepdims=True))
        out_ref[r, 8 * g : 8 * g + 8, :] = jnp.concatenate(best, axis=0) + norm_ref[buffer, 8 * g : 8 * g + 8, :]

    prepare(0, 0)
    for g in range(4):
        fetch_book(g).wait()

    def step(r, carry):
        for g in range(4):
            score(r, g, r % 2)
        prepare(jnp.minimum(r + 1, 3), (r + 1) % 2)
        send(r).start()
        return carry

    lax.fori_loop(0, 4, step, 0)
    for r in range(4):
        send(r).wait()


def join_kernel(got_hbm, old_hbm, out_hbm, got_ref, old_ref, out_ref, sem):
    loads = [
        pltpu.make_async_copy(src, dst, sem.at[i]) for i, (src, dst) in enumerate(((got_hbm, got_ref), (old_hbm, old_ref)))
    ]
    for load in loads:
        load.start()
    for load in loads:
        load.wait()
    weight = prior_weight + jnp.broadcast_to(got_ref[0, 192:193, :], (128, 128)).T
    low = iota((128, 128), 1) < 64
    for half in range(2):
        wide0, narrow0 = got_ref[2 * half, 0:128, :], unfold(got_ref[2 * half, 128:192, :])
        wide1, narrow1 = got_ref[2 * half + 1, 0:128, :], unfold(got_ref[2 * half + 1, 128:192, :])
        turned = pltpu.roll(wide1, 64, 1)
        sums = (wide0, jnp.where(low, narrow0, turned), jnp.where(low, turned, pltpu.roll(narrow1, 64, 1)))
        for i in range(3):
            at = 384 * half + 128 * i
            out_ref[:, at : at + 128] = (prior_weight * old_ref[:, at : at + 128] + sums[i]) / weight
    store = pltpu.make_async_copy(out_ref, out_hbm, sem.at[2])
    store.start()
    store.wait()


def call(kernel, out_shape, specs, out_specs, scratch=(), flops=0, moved=0, limit=LIMIT):
    return pl.pallas_call(
        kernel,
        out_shape=out_shape,
        in_specs=specs,
        out_specs=out_specs,
        scratch_shapes=scratch,
        compiler_params=pltpu.CompilerParams(vmem_limit_bytes=limit),
        cost_estimate=pl.CostEstimate(flops=flops, bytes_accessed=moved, transcendentals=0),
    )


def shape(*dims, dtype=F32):
    return jax.ShapeDtypeStruct(dims, dtype)


def pack_call(chunk, parts, destination, labels, embeddings):
    message, count = chunk["rows"], len(chunk["owners"])
    return call(
        functools.partial(pack_kernel, chunk, parts),
        shape(128 * message, 128),
        [HBM] * 3,
        HBM,
        [
            pltpu.VMEM((1, 512), jnp.int32),
            pltpu.VMEM((1, 512), jnp.int32),
            pltpu.VMEM((512, 768), F32),
            pltpu.VMEM((132 * message, 128), F32),
            pltpu.VMEM((1024, 768), BF16),
            pltpu.VMEM((2, 256 * count // parts, 768), F32),
            DMA((3 + parts,)),
        ],
        flops=2 * 256 * count * 512 * 768 * 2,
        moved=5 * 2**20,
    )(destination, labels, embeddings)


def exchange(chunk, outgoing):
    message = chunk["rows"]
    return lax.all_to_all(
        outgoing.reshape(128, 1, message * 128), ("shard", "rep"), split_axis=0, concat_axis=0, tiled=True
    ).reshape(128 * message, 128)


def score_call(rep, received, sums, book, olds):
    return call(
        score_kernel,
        shape(32, 4096),
        [SMEM] + [HBM] * 7,
        HBM,
        [
            pltpu.VMEM((128 * ALL["rows"], 128), F32),
            pltpu.VMEM((6160, 128), F32),
            pltpu.VMEM((4, 8, 128), F32),
            pltpu.VMEM((4, 200, 128), F32),
            pltpu.VMEM((32, 256, 256), BF16),
            pltpu.VMEM((4, 192, 128), F32),
            pltpu.VMEM((208, 128), F32),
            pltpu.VMEM((4, 384, 128), F32),
            pltpu.VMEM((2, 2, 192, 1024), BF16),
            pltpu.VMEM((2, 32, 1024), F32),
            pltpu.VMEM((4, 32, 1024), F32),
            DMA((22,)),
        ],
        flops=2**32,
        moved=2**23,
    )(rep, received, sums, book, *olds)


def local(embeddings, destination, labels, old_centroids, codebook):
    rep = lax.axis_index("rep").astype(jnp.int32).reshape(1)
    destination, labels = destination.reshape(1, 512), labels.reshape(1, 512)
    outgoing = pack_call(ALL, 4, destination, labels, embeddings)
    book = call(
        book_kernel, shape(32, 256, 256, dtype=BF16), [VMEM], VMEM, flops=2**28, moved=5 * 2**20
    )(jnp.transpose(codebook, (2, 0, 1)))

    old_centroids, book = lax.optimization_barrier((old_centroids, book))
    quarters = call(
        quarters_kernel, [shape(192, 128)] * 4, [SMEM, VMEM], [VMEM] * 4, flops=2**20, moved=2**20
    )(rep, old_centroids)
    olds = [quarters[0]]
    for step in (1, 2, 3):
        olds.append(lax.ppermute(quarters[step], "rep", [(i, (i + step) % 4) for i in range(4)]))

    received = exchange(ALL, outgoing)
    received, book = lax.optimization_barrier((received, book))
    sums = call(
        sums_kernel, shape(4, 200, 128), [VMEM], VMEM, flops=2**28, moved=2**22, limit=SUMS_LIMIT
    )(received)
    returned = lax.all_to_all(sums, "rep", split_axis=0, concat_axis=0, tiled=True)
    scores = score_call(rep, received, sums, book, olds)
    centroids = call(
        join_kernel,
        shape(128, 768),
        [HBM] * 2,
        HBM,
        [pltpu.VMEM((4, 200, 128), F32), pltpu.VMEM((128, 768), F32), pltpu.VMEM((128, 768), F32), DMA((3,))],
        flops=2**18,
        moved=2**20,
    )(returned, old_centroids)
    return (centroids, scores)


def solution(mesh):
    placed = (
        P(("shard", "rep"), None),
        P(("shard", "rep"), None),
        P(("shard", "rep")),
        P(("shard", "rep"), None),
        P("rep", None, None),
    )
    return jax.shard_map(
        local,
        mesh=mesh,
        in_specs=placed,
        out_specs=(P(("shard", "rep"), None), P("rep", "shard")),
        check_vma=False,
    )
```

time: 94.2 us -> 92.2 us (0.979)
  Pallas kernels: 39.8 us -> 37 us
    pallas_call x3, Pallas kernels: 29.2 us -> 26.4 us  [the longest x1 23.1 us: score_call(): call(score_kernel, shape(32, 4096), [SMEM] + [HBM] * 7, HBM, [pltpu.VMEM(...]
  transfers between devices with their start and end apart: 5 -> 5, of which waited for: 1 -> 1; matrix products, arithmetic and copies ran while one was open for 0% -> 0% of each run, Pallas kernels for 32% -> 33%
where the time goes in v3:
time: 92.2 us; the launch traced here: 91.8 us
  Pallas kernels  37 us (40%)
  waiting for transfers between devices  31.3 us (34%)
  starting transfers between devices  21.2 us (23%)
  local copies, waits for them, and re-layouts  1.47 us (2%)
    all_to_all x1, waiting for transfers between devices, exchange(): lax.all_to_all(outgoing.reshape(128, 1, message * 128), ('shard', 'rep'),...  31.3 us
    pallas_call x1, Pallas kernels, score_call(): call(score_kernel, shape(32, 4096), [SMEM] + [HBM] * 7, HBM, [pltpu.VMEM(...  23.1 us
    all_to_all x1, starting transfers between devices, exchange(): lax.all_to_all(outgoing.reshape(128, 1, message * 128), ('shard', 'rep'),...  11.5 us
    ppermute x3, starting transfers between devices, local(): lax.ppermute(quarters[step], 'rep', [(i, (i + step) % 4) for i in range(4)])  5.35 us
    pallas_call x1, Pallas kernels, pack_call(): call(functools.partial(pack_kernel, chunk, parts), shape(128 * message, 1...  4.49 us
    all_to_all x1, starting transfers between devices, local(): lax.all_to_all(sums, 'rep', split_axis=0, concat_axis=0, tiled=True)  4.3 us
    pallas_call x1, Pallas kernels, local(): call(book_kernel, shape(32, 256, 256, dtype=BF16), [VMEM], VMEM, flops=2...  4.15 us
    pallas_call x1, Pallas kernels, local(): call(join_kernel, shape(128, 768), [HBM] * 2, HBM, [pltpu.VMEM((4, 200, 1...  2.09 us
  transfers between devices with their start and end apart: 5, of which 1 were waited for; matrix products, arithmetic and copies ran while one was open for 0% of the time, Pallas kernels for 33%

profile of v3, /device:TPU:1, one launch (start us, length us, event | category | flops | bytes accessed | tf_op | source)
XLA Modules:
  0.0 91.8 jit_solution(16289419157861710888)
XLA Ops:
  0.6 4.5 %shard_map.68 = f32[6272,128]{1,0:T(8,128)} custom-call(s32[1,512]{1,0:T(1,128)} %bitcast.10, s32[1,512]{1,0:T(1,128)} %bitcast.11, f32[512,768]{1,0:T(8,128)} %rows_hbm.1), custom_call_target="tpu_custom_call" | custom-call | flops 1610612736 | bytes 5242880 | tf_op jit(solution)/shard_map/pallas_call | solution.py:348
  5.1 11.5 %all-to-all-start = ((f32[128,1,6272]{2,1,0:T(1,128)}), f32[128,1,6272]{2,1,0:T(1,128)S(1)}, u32[]{:S(2)}, u32[]{:S(2)}) async-start(f32[128,1,6272]{2,1,0:T(1,128)} %bitcast.8), calls=%async_computation | async-start | bytes 6422528 | tf_op jit(solution)/shard_map/all_to_all | solution.py:369
  16.6 4.2 %shard_map.69.book_hbm = bf16[32,256,256]{2,1,0:T(8,128)(2,1)} custom-call(f32[6,32,256]{2,1,0:T(8,128)} %bitcast.9), custom_call_target="tpu_custom_call" | custom-call | flops 268435456 | bytes 5242880 | tf_op jit(solution)/shard_map/pallas_call | solution.py:403
  20.8 1.9 %shard_map.72 = (f32[192,128]{1,0:T(8,128)}, f32[192,128]{1,0:T(8,128)}, f32[192,128]{1,0:T(8,128)}, f32[192,128]{1,0:T(8,128)}) custom-call(s32[1]{0:T(128)} %bitcast.5.rep_ref, f32[128,768]{1,0:T(8,128)} %old_ref), custom_call_target="tpu_custom_call" | custom-call | flops 1048576 | bytes 1048576 | tf_op jit(solution)/shard_map/pallas_call | solution.py:408
  22.7 1.5 %collective-permute-start = (f32[192,128]{1,0:T(8,128)}, f32[192,128]{1,0:T(8,128)S(1)}, u32[]{:S(2)}, u32[]{:S(2)}) collective-permute-start(f32[192,128]{1,0:T(8,128)} %get-tuple-element.15), channel_id=1, source_target_pairs={{0,1},{1,2},{2,3},{3,0},{4,5},{5,6},{6,7},{7,4},{8,9},{9,10},{10,1... | collective-permute-start | bytes 294920 | tf_op jit(solution)/shard_map/ppermute | solution.py:413
  24.2 2.9 %collective-permute-start.1 = (f32[192,128]{1,0:T(8,128)}, f32[192,128]{1,0:T(8,128)S(1)}, u32[]{:S(2)}, u32[]{:S(2)}) collective-permute-start(f32[192,128]{1,0:T(8,128)} %get-tuple-element.16), channel_id=1, source_target_pairs={{0,2},{1,3},{2,0},{3,1},{4,6},{5,7},{6,4},{7,5},{8,10},{9,11},{10,... | collective-permute-start | bytes 294920 | tf_op jit(solution)/shard_map/ppermute | solution.py:413
  27.2 0.9 collective-permute-start.2
  28.1 31.3 %all-to-all-done = f32[128,1,6272]{2,1,0:T(1,128)S(1)} async-done(((f32[128,1,6272]{2,1,0:T(1,128)}), f32[128,1,6272]{2,1,0:T(1,128)S(1)}, u32[]{:S(2)}, u32[]{:S(2)}) %all-to-all-start) | async-done | bytes 3211296 | tf_op jit(solution)/shard_map/all_to_all | solution.py:369
  59.4 0.0 copy-start
  59.4 1.2 %shard_map.70.sums_hbm = f32[4,200,128]{2,1,0:T(8,128)S(1)} custom-call(f32[6272,128]{1,0:T(8,128)S(1)} %bitcast.6), custom_call_target="tpu_custom_call" | custom-call | flops 268435456 | bytes 4194304 | tf_op jit(solution)/shard_map/pallas_call | solution.py:417
  60.6 0.0 copy-start.1
  60.6 0.8 copy-done.1
  61.4 4.3 %all-to-all-start.1 = ((f32[4,200,128]{2,1,0:T(8,128)}), f32[4,200,128]{2,1,0:T(8,128)}, u32[]{:S(2)}, u32[]{:S(2)}) async-start(f32[4,200,128]{2,1,0:T(8,128)} %copy-done.1), calls=%async_computation.1 | async-start | bytes 819200 | tf_op jit(solution)/shard_map/all_to_all | solution.py:420
  65.7 0.0 collective-permute-done.one_hbm
  65.7 0.0 copy-start.2
  65.7 0.0 collective-permute-done.1.two_hbm
  65.7 0.0 copy-start.3
  65.7 0.0 collective-permute-done.2.three_hbm
  65.7 0.0 copy-start.4
  65.8 0.0 copy-done
  65.8 0.6 copy-done.2
  66.3 0.1 copy-done.3
  66.4 0.1 copy-done.4
  66.4 23.1 %shard_map.73 = f32[32,4096]{1,0:T(8,128)} custom-call(s32[1]{0:T(128)} %bitcast.5.rep_ref, f32[6272,128]{1,0:T(8,128)} %bitcast.7, f32[4,200,128]{2,1,0:T(8,128)} %copy-done.1, bf16[32,256,256]{2,1,0:T(8,128)(2,1)} %shard_map.69.book_hbm, f32[192,128]{1,0:T(8,128)} %get-tuple-element.14.own_hbm, f32[192,128]{1,0:T(8,128)} %copy-done.2, ...), custom_call_target="tpu_custom_call" | custom-call | flops 4294967296 | bytes 8388608 | tf_op jit(solution)/shard_map/pallas_call | solution.py:375
  89.6 0.0 all-to-all-done.1.got_hbm
  89.6 2.1 %shard_map.71 = f32[128,768]{1,0:T(8,128)} custom-call(f32[4,200,128]{2,1,0:T(8,128)} %all-to-all-done.1.got_hbm, f32[128,768]{1,0:T(8,128)} %old_ref), custom_call_target="tpu_custom_call" | custom-call | flops 262144 | bytes 1048576 | tf_op jit(solution)/shard_map/pallas_call | solution.py:422
Async XLA Ops:
  5.1 54.3 %all-to-all-start = ((f32[128,1,6272]{2,1,0:T(1,128)}), f32[128,1,6272]{2,1,0:T(1,128)S(1)}, u32[]{:S(2)}, u32[]{:S(2)}) async-start(f32[128,1,6272]{2,1,0:T(1,128)} %bitcast.8), calls=%async_computation | async-start | bytes 6422528 | tf_op jit(solution)/shard_map/all_to_all | solution.py:369
  22.7 43.0 %collective-permute-start = (f32[192,128]{1,0:T(8,128)}, f32[192,128]{1,0:T(8,128)S(1)}, u32[]{:S(2)}, u32[]{:S(2)}) collective-permute-start(f32[192,128]{1,0:T(8,128)} %get-tuple-element.15), channel_id=1, source_target_pairs={{0,1},{1,2},{2,3},{3,0},{4,5},{5,6},{6,7},{7,4},{8,9},{9,10},{10,1... | collective-permute-start | bytes 294920 | tf_op jit(solution)/shard_map/ppermute | solution.py:413
  24.2 41.5 %collective-permute-start.1 = (f32[192,128]{1,0:T(8,128)}, f32[192,128]{1,0:T(8,128)S(1)}, u32[]{:S(2)}, u32[]{:S(2)}) collective-permute-start(f32[192,128]{1,0:T(8,128)} %get-tuple-element.16), channel_id=1, source_target_pairs={{0,2},{1,3},{2,0},{3,1},{4,6},{5,7},{6,4},{7,5},{8,10},{9,11},{10,... | collective-permute-start | bytes 294920 | tf_op jit(solution)/shard_map/ppermute | solution.py:413
  27.2 38.6 %collective-permute-start.2 = (f32[192,128]{1,0:T(8,128)}, f32[192,128]{1,0:T(8,128)S(1)}, u32[]{:S(2)}, u32[]{:S(2)}) collective-permute-start(f32[192,128]{1,0:T(8,128)} %get-tuple-element.17), channel_id=1, source_target_pairs={{0,3},{1,0},{2,1},{3,2},{4,7},{5,4},{6,5},{7,6},{8,11},{9,8},{10,9... | collective-permute-start | bytes 294920 | tf_op jit(solution)/shard_map/ppermute | solution.py:413
  59.4 6.4 %copy-start = (f32[128,1,6272]{2,1,0:T(1,128)}, f32[128,1,6272]{2,1,0:T(1,128)S(1)}, u32[]{:S(2)}) copy-start(f32[128,1,6272]{2,1,0:T(1,128)S(1)} %all-to-all-done) | copy-start | bytes 9633796
  60.6 0.8 copy-start.1
  61.4 28.2 %all-to-all-start.1 = ((f32[4,200,128]{2,1,0:T(8,128)}), f32[4,200,128]{2,1,0:T(8,128)}, u32[]{:S(2)}, u32[]{:S(2)}) async-start(f32[4,200,128]{2,1,0:T(8,128)} %copy-done.1), calls=%async_computation.1 | async-start | bytes 819200 | tf_op jit(solution)/shard_map/all_to_all | solution.py:420
  65.7 0.6 copy-start.2
  65.7 0.7 copy-start.3
  65.7 0.7 copy-start.4

commit v4 on v3

--- a/solution.py
+++ b/solution.py
@@ -15,6 +15,8 @@
 DMA = pltpu.SemaphoreType.DMA
 LIMIT = 58 * 2**20
 SUMS_LIMIT = 24 * 2**20
+SCORE_LIMIT = 51 * 2**20
+JOIN_LIMIT = 16 * 2**20
 
 ALL = {"owners": (0, 1, 2, 3), "narrow": (((0, 1), 33), ((2, 3), 41)), "labels": 0, "wide": 1, "rows": 49}
 
@@ -173,7 +175,7 @@
     return jnp.concatenate([got_ref[pl.ds(ALL["rows"] * q + offset, 8), :] for q in range(16 * c, 16 * c + 16)], axis=0)
 
 
-def sums_kernel(got_ref, sums_ref):
+def sums_kernel(rep_ref, got_ref, sums_ref, one_ref, two_ref, three_ref):
     posting = iota((128, 128), 0).astype(F32)
     lab = label_rows(got_ref)
     sums = [None] * 4
@@ -202,6 +204,8 @@
             sums_ref[r, 0:128, :] = sums[r][:, 0:128]
             sums_ref[r, 128:192, :] = fold(tail)
             sums_ref[r, 192:200, :] = jnp.broadcast_to(jnp.sum(counts[r].T, axis=0, keepdims=True), (8, 128))
+    for step, ref in ((1, one_ref), (2, two_ref), (3, three_ref)):
+        ref[...] = sums_ref[lax.rem(rep_ref[0] + step, 4)]
 
 
 def score_kernel(
@@ -254,8 +258,9 @@
                     at = 192 * piece + 48 * g + 8 * t
                     cent_ref[r, at : at + 8, :] = block.astype(F32)
 
-    def prepare(r, buffer):
+    def prepare(r, half, buffer):
         labs = lab_ref[r]
+        lanes = slice(1024 * half, 1024 * half + 1024)
         posting = iota((128, 128), 0).astype(F32)
         hot = jnp.concatenate([(posting == labs[c : c + 1]).astype(BF16) for c in range(8)], axis=1)
         near = dot(cent_ref[r].astype(BF16), hot)
@@ -271,11 +276,11 @@
                 axis=0,
             )
             res = rows - (near[span] + near[192 + 48 * g : 240 + 48 * g])
-            norm_ref[buffer, 8 * g : 8 * g + 8, :] = jnp.sum((res * res).reshape(6, 8, 1024), axis=0)
+            norm_ref[buffer, 8 * g : 8 * g + 8, lanes] = jnp.sum((res * res).reshape(6, 8, 1024), axis=0)
             for i, piece in enumerate(split2(res)):
-                piece_ref[buffer, i, span, :] = piece
-
-    ones = jnp.where(iota((16, 1024), 0) < 3, 1.0, 0.0).astype(BF16)
+                piece_ref[buffer, i, span, lanes] = piece
+
+    ones = jnp.where(iota((16, 2048), 0) < 3, 1.0, 0.0).astype(BF16)
 
     def score(r, g, buffer):
         first = piece_ref[buffer, 0, 48 * g : 48 * g + 48, :]
@@ -284,30 +289,35 @@
         best = []
         for m in range(8):
             value = dot(book_ref[8 * g + m], right)
-            value = jnp.min(value.reshape(32, 8, 1024), axis=0)
+            value = jnp.min(value.reshape(32, 8, 2048), axis=0)
             best.append(jnp.min(value, axis=0, keepdims=True))
-        out_ref[r, 8 * g : 8 * g + 8, :] = jnp.concatenate(best, axis=0) + norm_ref[buffer, 8 * g : 8 * g + 8, :]
-
-    prepare(0, 0)
+        result = jnp.concatenate(best, axis=0) + norm_ref[buffer, 8 * g : 8 * g + 8, :]
+        out_ref[r, 8 * g : 8 * g + 8, :] = result[:, 0:1024]
+        out_ref[r + 1, 8 * g : 8 * g + 8, :] = result[:, 1024:2048]
+
+    prepare(0, 0, 0)
+    prepare(1, 1, 0)
     for g in range(4):
         fetch_book(g).wait()
-
-    def step(r, carry):
+    for pair in range(2):
         for g in range(4):
-            score(r, g, r % 2)
-        prepare(jnp.minimum(r + 1, 3), (r + 1) % 2)
-        send(r).start()
-        return carry
-
-    lax.fori_loop(0, 4, step, 0)
+            score(2 * pair, g, pair)
+        if pair == 0:
+            prepare(2, 0, 1)
+            prepare(3, 1, 1)
+        send(2 * pair).start()
+        send(2 * pair + 1).start()
     for r in range(4):
         send(r).wait()
 
 
-def join_kernel(got_hbm, old_hbm, out_hbm, got_ref, old_ref, out_ref, sem):
-    loads = [
-        pltpu.make_async_copy(src, dst, sem.at[i]) for i, (src, dst) in enumerate(((got_hbm, got_ref), (old_hbm, old_ref)))
-    ]
+def join_kernel(
+    rep_ref, own_hbm, one_hbm, two_hbm, three_hbm, old_hbm, out_hbm, got_ref, old_ref, out_ref, sem
+):
+    rep = rep_ref[0]
+    pairs = [(own_hbm.at[rep], got_ref.at[0]), (old_hbm, old_ref)]
+    pairs += [(src, got_ref.at[i + 1]) for i, src in enumerate((one_hbm, two_hbm, three_hbm))]
+    loads = [pltpu.make_async_copy(src, dst, sem.at[i]) for i, (src, dst) in enumerate(pairs)]
     for load in loads:
         load.start()
     for load in loads:
@@ -315,14 +325,15 @@
     weight = prior_weight + jnp.broadcast_to(got_ref[0, 192:193, :], (128, 128)).T
     low = iota((128, 128), 1) < 64
     for half in range(2):
-        wide0, narrow0 = got_ref[2 * half, 0:128, :], unfold(got_ref[2 * half, 128:192, :])
-        wide1, narrow1 = got_ref[2 * half + 1, 0:128, :], unfold(got_ref[2 * half + 1, 128:192, :])
+        even, odd = lax.rem(rep - 2 * half + 4, 4), lax.rem(rep - 2 * half + 3, 4)
+        wide0, narrow0 = got_ref[even, 0:128, :], unfold(got_ref[even, 128:192, :])
+        wide1, narrow1 = got_ref[odd, 0:128, :], unfold(got_ref[odd, 128:192, :])
         turned = pltpu.roll(wide1, 64, 1)
         sums = (wide0, jnp.where(low, narrow0, turned), jnp.where(low, turned, pltpu.roll(narrow1, 64, 1)))
         for i in range(3):
             at = 384 * half + 128 * i
             out_ref[:, at : at + 128] = (prior_weight * old_ref[:, at : at + 128] + sums[i]) / weight
-    store = pltpu.make_async_copy(out_ref, out_hbm, sem.at[2])
+    store = pltpu.make_async_copy(out_ref, out_hbm, sem.at[5])
     store.start()
     store.wait()
 
@@ -386,13 +397,14 @@
             pltpu.VMEM((4, 192, 128), F32),
             pltpu.VMEM((208, 128), F32),
             pltpu.VMEM((4, 384, 128), F32),
-            pltpu.VMEM((2, 2, 192, 1024), BF16),
-            pltpu.VMEM((2, 32, 1024), F32),
+            pltpu.VMEM((2, 2, 192, 2048), BF16),
+            pltpu.VMEM((2, 32, 2048), F32),
             pltpu.VMEM((4, 32, 1024), F32),
             DMA((22,)),
         ],
         flops=2**32,
         moved=2**23,
+        limit=SCORE_LIMIT,
     )(rep, received, sums, book, *olds)
 
 
@@ -414,20 +426,29 @@
 
     received = exchange(ALL, outgoing)
     received, book = lax.optimization_barrier((received, book))
-    sums = call(
-        sums_kernel, shape(4, 200, 128), [VMEM], VMEM, flops=2**28, moved=2**22, limit=SUMS_LIMIT
-    )(received)
-    returned = lax.all_to_all(sums, "rep", split_axis=0, concat_axis=0, tiled=True)
+    sums, *sent = call(
+        sums_kernel,
+        [shape(4, 200, 128)] + [shape(200, 128)] * 3,
+        [SMEM, VMEM],
+        [VMEM] * 4,
+        flops=2**28,
+        moved=2**22,
+        limit=SUMS_LIMIT,
+    )(rep, received)
+    returned = [
+        lax.ppermute(sent[step - 1], "rep", [(i, (i + step) % 4) for i in range(4)]) for step in (1, 2, 3)
+    ]
     scores = score_call(rep, received, sums, book, olds)
     centroids = call(
         join_kernel,
         shape(128, 768),
-        [HBM] * 2,
+        [SMEM] + [HBM] * 5,
         HBM,
-        [pltpu.VMEM((4, 200, 128), F32), pltpu.VMEM((128, 768), F32), pltpu.VMEM((128, 768), F32), DMA((3,))],
+        [pltpu.VMEM((4, 200, 128), F32), pltpu.VMEM((128, 768), F32), pltpu.VMEM((128, 768), F32), DMA((6,))],
         flops=2**18,
         moved=2**20,
-    )(returned, old_centroids)
+        limit=JOIN_LIMIT,
+    )(rep, sums, *returned, old_centroids)
     return (centroids, scores)
 
 

time: 92.2 us -> 88.7 us (0.962)
  local copies, waits for them, and re-layouts: 1.47 us -> 0.01 us
  starting transfers between devices: 21.2 us -> 20 us
    all_to_all x1 -> x0, starting transfers between devices: 4.3 us -> none  [local(): lax.all_to_all(sums, 'rep', split_axis=0, concat_axis=0, tiled=True)]
    ppermute x0 -> x3, starting transfers between devices: none -> 3.11 us  [local(): lax.ppermute(sent[step - 1], 'rep', [(i, (i + step) % 4) for i in range(4)])]
    unnamed x10 -> x6, local copies, waits for them, and re-layouts: 1.47 us -> 0.01 us
  transfers between devices with their start and end apart: 5 -> 7, of which waited for: 1 -> 1; matrix products, arithmetic and copies ran while one was open for 0% -> 0% of each run, Pallas kernels for 33% -> 34%
where the time goes in v4:
time: 88.7 us; the launch traced here: 88.4 us
  Pallas kernels  36.2 us (41%)
  waiting for transfers between devices  31.3 us (35%)
  starting transfers between devices  20 us (23%)
  between operations  0.9 us (1%)
    all_to_all x1, waiting for transfers between devices, exchange(): lax.all_to_all(outgoing.reshape(128, 1, message * 128), ('shard', 'rep'),...  31.3 us
    pallas_call x1, Pallas kernels, score_call(): call(score_kernel, shape(32, 4096), [SMEM] + [HBM] * 7, HBM, [pltpu.VMEM(...  22.7 us
    all_to_all x1, starting transfers between devices, exchange(): lax.all_to_all(outgoing.reshape(128, 1, message * 128), ('shard', 'rep'),...  11.5 us
    ppermute x3, starting transfers between devices, local(): lax.ppermute(quarters[step], 'rep', [(i, (i + step) % 4) for i in range(4)])  5.35 us
    pallas_call x1, Pallas kernels, pack_call(): call(functools.partial(pack_kernel, chunk, parts), shape(128 * message, 1...  4.49 us
    pallas_call x1, Pallas kernels, local(): call(book_kernel, shape(32, 256, 256, dtype=BF16), [VMEM], VMEM, flops=2...  4.15 us
    ppermute x3, starting transfers between devices, local(): lax.ppermute(sent[step - 1], 'rep', [(i, (i + step) % 4) for i in range(4)])  3.11 us
    pallas_call x1, Pallas kernels, local(): call(quarters_kernel, [shape(192, 128)] * 4, [SMEM, VMEM], [VMEM] * 4, fl...  1.92 us
  transfers between devices with their start and end apart: 7, of which 1 were waited for; matrix products, arithmetic and copies ran while one was open for 0% of the time, Pallas kernels for 34%

profile of v4, /device:TPU:1, one launch (start us, length us, event | category | flops | bytes accessed | tf_op | source)
XLA Modules:
  0.0 88.4 jit_solution(11256277144565001389)
XLA Ops:
  0.6 4.5 %shard_map.68 = f32[6272,128]{1,0:T(8,128)} custom-call(s32[1,512]{1,0:T(1,128)} %bitcast.10, s32[1,512]{1,0:T(1,128)} %bitcast.11, f32[512,768]{1,0:T(8,128)} %rows_hbm.1), custom_call_target="tpu_custom_call" | custom-call | flops 1610612736 | bytes 5242880 | tf_op jit(solution)/shard_map/pallas_call | solution.py:359
  5.1 11.5 %all-to-all-start = ((f32[128,1,6272]{2,1,0:T(1,128)}), f32[128,1,6272]{2,1,0:T(1,128)S(1)}, u32[]{:S(2)}, u32[]{:S(2)}) async-start(f32[128,1,6272]{2,1,0:T(1,128)} %bitcast.8), calls=%async_computation | async-start | bytes 6422528 | tf_op jit(solution)/shard_map/all_to_all | solution.py:380
  16.6 4.2 %shard_map.69.book_hbm = bf16[32,256,256]{2,1,0:T(8,128)(2,1)} custom-call(f32[6,32,256]{2,1,0:T(8,128)} %bitcast.9), custom_call_target="tpu_custom_call" | custom-call | flops 268435456 | bytes 5242880 | tf_op jit(solution)/shard_map/pallas_call | solution.py:415
  20.8 1.9 %shard_map.72 = (f32[192,128]{1,0:T(8,128)}, f32[192,128]{1,0:T(8,128)}, f32[192,128]{1,0:T(8,128)}, f32[192,128]{1,0:T(8,128)}) custom-call(s32[1]{0:T(128)} %bitcast.rep_ref, f32[128,768]{1,0:T(8,128)} %old_ref), custom_call_target="tpu_custom_call" | custom-call | flops 1048576 | bytes 1048576 | tf_op jit(solution)/shard_map/pallas_call | solution.py:420
  22.7 0.0 copy-start.2
  22.7 1.5 %collective-permute-start.3 = (f32[192,128]{1,0:T(8,128)}, f32[192,128]{1,0:T(8,128)S(1)}, u32[]{:S(2)}, u32[]{:S(2)}) collective-permute-start(f32[192,128]{1,0:T(8,128)} %get-tuple-element.23), channel_id=1, source_target_pairs={{0,1},{1,2},{2,3},{3,0},{4,5},{5,6},{6,7},{7,4},{8,9},{9,10},{10,1... | collective-permute-start | bytes 294920 | tf_op jit(solution)/shard_map/ppermute | solution.py:425
  24.2 2.9 %collective-permute-start.4 = (f32[192,128]{1,0:T(8,128)}, f32[192,128]{1,0:T(8,128)S(1)}, u32[]{:S(2)}, u32[]{:S(2)}) collective-permute-start(f32[192,128]{1,0:T(8,128)} %get-tuple-element.24), channel_id=1, source_target_pairs={{0,2},{1,3},{2,0},{3,1},{4,6},{5,7},{6,4},{7,5},{8,10},{9,11},{10,... | collective-permute-start | bytes 294920 | tf_op jit(solution)/shard_map/ppermute | solution.py:425
  27.2 0.9 %collective-permute-start.5 = (f32[192,128]{1,0:T(8,128)}, f32[192,128]{1,0:T(8,128)}, u32[]{:S(2)}, u32[]{:S(2)}) collective-permute-start(f32[192,128]{1,0:T(8,128)} %get-tuple-element.25), channel_id=1, source_target_pairs={{0,3},{1,0},{2,1},{3,2},{4,7},{5,4},{6,5},{7,6},{8,11},{9,8},{10,9... | collective-permute-start | bytes 294920 | tf_op jit(solution)/shard_map/ppermute | solution.py:425
  28.1 31.3 %all-to-all-done = f32[128,1,6272]{2,1,0:T(1,128)S(1)} async-done(((f32[128,1,6272]{2,1,0:T(1,128)}), f32[128,1,6272]{2,1,0:T(1,128)S(1)}, u32[]{:S(2)}, u32[]{:S(2)}) %all-to-all-start) | async-done | bytes 3211296 | tf_op jit(solution)/shard_map/all_to_all | solution.py:380
  59.4 0.0 copy-start
  59.4 1.2 %shard_map.70 = (f32[4,200,128]{2,1,0:T(8,128)S(1)}, f32[200,128]{1,0:T(8,128)S(1)}, f32[200,128]{1,0:T(8,128)S(1)}, f32[200,128]{1,0:T(8,128)S(1)}) custom-call(s32[1]{0:T(128)} %bitcast.rep_ref, f32[6272,128]{1,0:T(8,128)S(1)} %bitcast.6), custom_call_target="tpu_custom_call" | custom-call | flops 268435456 | bytes 4194304 | tf_op jit(solution)/shard_map/pallas_call | solution.py:429
  60.6 0.6 collective-permute-start
  61.3 0.6 collective-permute-start.1
  61.9 0.0 collective-permute-done.3.one_hbm
  61.9 1.9 %collective-permute-start.2 = (f32[200,128]{1,0:T(8,128)S(1)}, f32[200,128]{1,0:T(8,128)S(1)}, u32[]{:S(2)}, u32[]{:S(2)}) collective-permute-start(f32[200,128]{1,0:T(8,128)S(1)} %get-tuple-element.19), channel_id=1, source_target_pairs={{0,3},{1,0},{2,1},{3,2},{4,7},{5,4},{6,5},{7,6},{8,11},{9,8},{10,9... | collective-permute-start | bytes 307208 | tf_op jit(solution)/shard_map/ppermute | solution.py:439
  63.7 0.0 collective-permute-done.4.two_hbm
  63.7 0.0 collective-permute-done.5.three_hbm
  63.7 0.0 copy-done
  63.8 0.0 copy-done.2
  63.8 0.0 copy-start.1
  63.8 22.7 %shard_map.73 = f32[32,4096]{1,0:T(8,128)} custom-call(s32[1]{0:T(128)} %bitcast.rep_ref, f32[6272,128]{1,0:T(8,128)} %bitcast.7, f32[4,200,128]{2,1,0:T(8,128)S(1)} %get-tuple-element.16.own_hbm.sums_hbm, bf16[32,256,256]{2,1,0:T(8,128)(2,1)} %shard_map.69.book_hbm, f32[192,128]{1,0:T(8,128)S(1)} %copy-done.2, ...), custom_call_target="tpu_custom_call" | custom-call | flops 4294967296 | bytes 8388608 | tf_op jit(solution)/shard_map/pallas_call | solution.py:386
  86.4 0.0 collective-permute-done.one_hbm
  86.5 0.0 collective-permute-done.1.two_hbm
  86.5 0.0 collective-permute-done.2.three_hbm
  86.5 0.0 copy-done.1
  86.5 1.7 %shard_map.71 = f32[128,768]{1,0:T(8,128)} custom-call(s32[1]{0:T(128)} %bitcast.rep_ref, f32[4,200,128]{2,1,0:T(8,128)S(1)} %get-tuple-element.16.own_hbm.sums_hbm, f32[200,128]{1,0:T(8,128)S(1)} %collective-permute-done.one_hbm, f32[200,128]{1,0:T(8,128)S(1)} %collective-permute-done.1.two_hbm, f32[200,128]{1,0:T(8,128)S(1)} %collective-permute-done.2.three_hbm, ...), custom_call_target="tpu_custom_call" | custom-call | flops 262144 | bytes 1048576 | tf_op jit(solution)/shard_map/pallas_call | solution.py:442
Async XLA Ops:
  5.1 54.3 %all-to-all-start = ((f32[128,1,6272]{2,1,0:T(1,128)}), f32[128,1,6272]{2,1,0:T(1,128)S(1)}, u32[]{:S(2)}, u32[]{:S(2)}) async-start(f32[128,1,6272]{2,1,0:T(1,128)} %bitcast.8), calls=%async_computation | async-start | bytes 6422528 | tf_op jit(solution)/shard_map/all_to_all | solution.py:380
  22.7 41.0 %copy-start.2 = (f32[192,128]{1,0:T(8,128)S(1)}, f32[192,128]{1,0:T(8,128)}, u32[]{:S(2)}) copy-start(f32[192,128]{1,0:T(8,128)} %get-tuple-element.22.own_hbm) | copy-start | bytes 294916
  22.7 39.1 %collective-permute-start.3 = (f32[192,128]{1,0:T(8,128)}, f32[192,128]{1,0:T(8,128)S(1)}, u32[]{:S(2)}, u32[]{:S(2)}) collective-permute-start(f32[192,128]{1,0:T(8,128)} %get-tuple-element.23), channel_id=1, source_target_pairs={{0,1},{1,2},{2,3},{3,0},{4,5},{5,6},{6,7},{7,4},{8,9},{9,10},{10,1... | collective-permute-start | bytes 294920 | tf_op jit(solution)/shard_map/ppermute | solution.py:425
  24.2 39.5 %collective-permute-start.4 = (f32[192,128]{1,0:T(8,128)}, f32[192,128]{1,0:T(8,128)S(1)}, u32[]{:S(2)}, u32[]{:S(2)}) collective-permute-start(f32[192,128]{1,0:T(8,128)} %get-tuple-element.24), channel_id=1, source_target_pairs={{0,2},{1,3},{2,0},{3,1},{4,6},{5,7},{6,4},{7,5},{8,10},{9,11},{10,... | collective-permute-start | bytes 294920 | tf_op jit(solution)/shard_map/ppermute | solution.py:425
  27.2 36.6 %collective-permute-start.5 = (f32[192,128]{1,0:T(8,128)}, f32[192,128]{1,0:T(8,128)}, u32[]{:S(2)}, u32[]{:S(2)}) collective-permute-start(f32[192,128]{1,0:T(8,128)} %get-tuple-element.25), channel_id=1, source_target_pairs={{0,3},{1,0},{2,1},{3,2},{4,7},{5,4},{6,5},{7,6},{8,11},{9,8},{10,9... | collective-permute-start | bytes 294920 | tf_op jit(solution)/shard_map/ppermute | solution.py:425
  59.4 4.3 %copy-start = (f32[128,1,6272]{2,1,0:T(1,128)}, f32[128,1,6272]{2,1,0:T(1,128)S(1)}, u32[]{:S(2)}) copy-start(f32[128,1,6272]{2,1,0:T(1,128)S(1)} %all-to-all-done) | copy-start | bytes 9633796
  60.6 25.8 %collective-permute-start = (f32[200,128]{1,0:T(8,128)S(1)}, f32[200,128]{1,0:T(8,128)S(1)}, u32[]{:S(2)}, u32[]{:S(2)}) collective-permute-start(f32[200,128]{1,0:T(8,128)S(1)} %get-tuple-element.17), channel_id=1, source_target_pairs={{0,1},{1,2},{2,3},{3,0},{4,5},{5,6},{6,7},{7,4},{8,9},{9,10},{10,1... | collective-permute-start | bytes 307208 | tf_op jit(solution)/shard_map/ppermute | solution.py:439
  61.3 25.2 %collective-permute-start.1 = (f32[200,128]{1,0:T(8,128)S(1)}, f32[200,128]{1,0:T(8,128)S(1)}, u32[]{:S(2)}, u32[]{:S(2)}) collective-permute-start(f32[200,128]{1,0:T(8,128)S(1)} %get-tuple-element.18), channel_id=1, source_target_pairs={{0,2},{1,3},{2,0},{3,1},{4,6},{5,7},{6,4},{7,5},{8,10},{9,11},{10,... | collective-permute-start | bytes 307208 | tf_op jit(solution)/shard_map/ppermute | solution.py:439
  61.9 24.6 %collective-permute-start.2 = (f32[200,128]{1,0:T(8,128)S(1)}, f32[200,128]{1,0:T(8,128)S(1)}, u32[]{:S(2)}, u32[]{:S(2)}) collective-permute-start(f32[200,128]{1,0:T(8,128)S(1)} %get-tuple-element.19), channel_id=1, source_target_pairs={{0,3},{1,0},{2,1},{3,2},{4,7},{5,4},{6,5},{7,6},{8,11},{9,8},{10,9... | collective-permute-start | bytes 307208 | tf_op jit(solution)/shard_map/ppermute | solution.py:439
  63.8 22.7 %copy-start.1 = (f32[128,768]{1,0:T(8,128)S(1)}, f32[128,768]{1,0:T(8,128)}, u32[]{:S(2)}) copy-start(f32[128,768]{1,0:T(8,128)} %old_ref) | copy-start | bytes 1179652

commit v5 on v4

--- a/solution.py
+++ b/solution.py
@@ -15,7 +15,7 @@
 DMA = pltpu.SemaphoreType.DMA
 LIMIT = 58 * 2**20
 SUMS_LIMIT = 24 * 2**20
-SCORE_LIMIT = 51 * 2**20
+SCORE_LIMIT = 48 * 2**20
 JOIN_LIMIT = 16 * 2**20
 
 ALL = {"owners": (0, 1, 2, 3), "narrow": (((0, 1), 33), ((2, 3), 41)), "labels": 0, "wide": 1, "rows": 49}
@@ -209,8 +209,8 @@
 
 
 def score_kernel(
-    rep_ref, got_hbm, sums_hbm, book_hbm, own_hbm, one_hbm, two_hbm, three_hbm, out_hbm,
-    got_ref, work_ref, lab_ref, sums_ref, book_ref, old_ref, flip_ref, cent_ref, piece_ref, norm_ref, out_ref, sem,
+    rep_ref, got_ref, sums_hbm, book_hbm, own_hbm, one_hbm, two_hbm, three_hbm, out_hbm,
+    work_ref, lab_ref, sums_ref, book_ref, old_ref, flip_ref, cent_ref, piece_ref, norm_ref, out_ref, sem,
 ):
     def fetch(src, dst, at):
         return pltpu.make_async_copy(src, dst, sem.at[at])
@@ -218,15 +218,10 @@
     def fetch_book(g):
         return fetch(book_hbm.at[pl.ds(8 * g, 8)], book_ref.at[pl.ds(8 * g, 8)], 4 + g)
 
-    def send(r):
-        span = pl.ds(pl.multiple_of(1024 * r, 1024), 1024)
-        return fetch(out_ref.at[r], out_hbm.at[:, span], 14 + r)
-
-    rows = []
-    for i in range(4):
-        span = pl.ds(32 * ALL["rows"] * i, 32 * ALL["rows"])
-        rows.append(fetch(got_hbm.at[span], got_ref.at[span], 18 + i))
-        rows[i].start()
+    def send(g):
+        span = pl.ds(8 * g, 8)
+        return fetch(out_ref.at[span], out_hbm.at[span], 14 + g)
+
     small = [fetch(sums_hbm, sums_ref, 8)]
     small += [fetch(src, old_ref.at[i], 10 + i) for i, src in enumerate((own_hbm, one_hbm, two_hbm, three_hbm))]
     for copy in small:
@@ -235,8 +230,6 @@
         fetch_book(g).start()
     rep = rep_ref[0]
     for c in range(8):
-        if c % 2 == 0:
-            rows[c // 2].wait()
         for members, offset in ALL["narrow"]:
             narrow = tile_rows(got_ref, c, offset).T
             for k, r in enumerate(members):
@@ -258,9 +251,9 @@
                     at = 192 * piece + 48 * g + 8 * t
                     cent_ref[r, at : at + 8, :] = block.astype(F32)
 
-    def prepare(r, half, buffer):
+    def prepare(r):
         labs = lab_ref[r]
-        lanes = slice(1024 * half, 1024 * half + 1024)
+        lanes = slice(1024 * r, 1024 * r + 1024)
         posting = iota((128, 128), 0).astype(F32)
         hot = jnp.concatenate([(posting == labs[c : c + 1]).astype(BF16) for c in range(8)], axis=1)
         near = dot(cent_ref[r].astype(BF16), hot)
@@ -276,39 +269,32 @@
                 axis=0,
             )
             res = rows - (near[span] + near[192 + 48 * g : 240 + 48 * g])
-            norm_ref[buffer, 8 * g : 8 * g + 8, lanes] = jnp.sum((res * res).reshape(6, 8, 1024), axis=0)
+            norm_ref[8 * g : 8 * g + 8, lanes] = jnp.sum((res * res).reshape(6, 8, 1024), axis=0)
             for i, piece in enumerate(split2(res)):
-                piece_ref[buffer, i, span, lanes] = piece
-
-    ones = jnp.where(iota((16, 2048), 0) < 3, 1.0, 0.0).astype(BF16)
-
-    def score(r, g, buffer):
-        first = piece_ref[buffer, 0, 48 * g : 48 * g + 48, :]
-        second = piece_ref[buffer, 1, 48 * g : 48 * g + 48, :]
+                piece_ref[i, span, lanes] = piece
+
+    ones = jnp.where(iota((16, 4096), 0) < 3, 1.0, 0.0).astype(BF16)
+
+    def score(g):
+        first = piece_ref[0, 48 * g : 48 * g + 48, :]
+        second = piece_ref[1, 48 * g : 48 * g + 48, :]
         right = jnp.concatenate([first, first, first, second, second, ones], axis=0)
         best = []
         for m in range(8):
             value = dot(book_ref[8 * g + m], right)
-            value = jnp.min(value.reshape(32, 8, 2048), axis=0)
+            value = jnp.min(value.reshape(32, 8, 4096), axis=0)
             best.append(jnp.min(value, axis=0, keepdims=True))
-        result = jnp.concatenate(best, axis=0) + norm_ref[buffer, 8 * g : 8 * g + 8, :]
-        out_ref[r, 8 * g : 8 * g + 8, :] = result[:, 0:1024]
-        out_ref[r + 1, 8 * g : 8 * g + 8, :] = result[:, 1024:2048]
-
-    prepare(0, 0, 0)
-    prepare(1, 1, 0)
+        out_ref[8 * g : 8 * g + 8, :] = jnp.concatenate(best, axis=0) + norm_ref[8 * g : 8 * g + 8, :]
+
+    for r in range(4):
+        prepare(r)
     for g in range(4):
         fetch_book(g).wait()
-    for pair in range(2):
-        for g in range(4):
-            score(2 * pair, g, pair)
-        if pair == 0:
-            prepare(2, 0, 1)
-            prepare(3, 1, 1)
-        send(2 * pair).start()
-        send(2 * pair + 1).start()
-    for r in range(4):
-        send(r).wait()
+    for g in range(4):
+        score(g)
+        send(g).start()
+    for g in range(4):
+        send(g).wait()
 
 
 def join_kernel(
@@ -386,10 +372,9 @@
     return call(
         score_kernel,
         shape(32, 4096),
-        [SMEM] + [HBM] * 7,
+        [SMEM, VMEM] + [HBM] * 6,
         HBM,
         [
-            pltpu.VMEM((128 * ALL["rows"], 128), F32),
             pltpu.VMEM((6160, 128), F32),
             pltpu.VMEM((4, 8, 128), F32),
             pltpu.VMEM((4, 200, 128), F32),
@@ -397,9 +382,9 @@
             pltpu.VMEM((4, 192, 128), F32),
             pltpu.VMEM((208, 128), F32),
             pltpu.VMEM((4, 384, 128), F32),
-            pltpu.VMEM((2, 2, 192, 2048), BF16),
-            pltpu.VMEM((2, 32, 2048), F32),
-            pltpu.VMEM((4, 32, 1024), F32),
+            pltpu.VMEM((2, 192, 4096), BF16),
+            pltpu.VMEM((32, 4096), F32),
+            pltpu.VMEM((32, 4096), F32),
             DMA((22,)),
         ],
         flops=2**32,

time: 88.7 us -> 87.8 us (0.990)
  Pallas kernels: 36.2 us -> 35.3 us
    pallas_call x1, Pallas kernels: 22.7 us -> 21.8 us  [score_call(): call(score_kernel, shape(32, 4096), [SMEM, VMEM] + [HBM] * 6, HBM, [pltpu...]
  transfers between devices with their start and end apart: 7 -> 7, of which waited for: 1 -> 1; matrix products, arithmetic and copies ran while one was open for 0% -> 0% of each run, Pallas kernels for 34% -> 33%
where the time goes in v5:
time: 87.8 us; the launch traced here: 87.5 us
  Pallas kernels  35.3 us (40%)
  waiting for transfers between devices  31.3 us (36%)
  starting transfers between devices  20 us (23%)
  between operations  0.89 us (1%)
    all_to_all x1, waiting for transfers between devices, exchange(): lax.all_to_all(outgoing.reshape(128, 1, message * 128), ('shard', 'rep'),...  31.3 us
    pallas_call x1, Pallas kernels, score_call(): call(score_kernel, shape(32, 4096), [SMEM, VMEM] + [HBM] * 6, HBM, [pltpu...  21.8 us
    all_to_all x1, starting transfers between devices, exchange(): lax.all_to_all(outgoing.reshape(128, 1, message * 128), ('shard', 'rep'),...  11.5 us
    ppermute x3, starting transfers between devices, local(): lax.ppermute(quarters[step], 'rep', [(i, (i + step) % 4) for i in range(4)])  5.35 us
    pallas_call x1, Pallas kernels, pack_call(): call(functools.partial(pack_kernel, chunk, parts), shape(128 * message, 1...  4.5 us
    pallas_call x1, Pallas kernels, local(): call(book_kernel, shape(32, 256, 256, dtype=BF16), [VMEM], VMEM, flops=2...  4.16 us
    ppermute x3, starting transfers between devices, local(): lax.ppermute(sent[step - 1], 'rep', [(i, (i + step) % 4) for i in range(4)])  3.11 us
    pallas_call x1, Pallas kernels, local(): call(quarters_kernel, [shape(192, 128)] * 4, [SMEM, VMEM], [VMEM] * 4, fl...  1.92 us
  transfers between devices with their start and end apart: 7, of which 1 were waited for; matrix products, arithmetic and copies ran while one was open for 0% of the time, Pallas kernels for 33%

profile of v5, /device:TPU:1, one launch (start us, length us, event | category | flops | bytes accessed | tf_op | source)
XLA Modules:
  0.0 87.5 jit_solution(10232035499459784787)
XLA Ops:
  0.6 4.5 %shard_map.68 = f32[6272,128]{1,0:T(8,128)} custom-call(s32[1,512]{1,0:T(1,128)} %bitcast.10, s32[1,512]{1,0:T(1,128)} %bitcast.11, f32[512,768]{1,0:T(8,128)} %rows_hbm.1), custom_call_target="tpu_custom_call" | custom-call | flops 1610612736 | bytes 5242880 | tf_op jit(solution)/shard_map/pallas_call | solution.py:345
  5.1 11.5 %all-to-all-start = ((f32[128,1,6272]{2,1,0:T(1,128)}), f32[128,1,6272]{2,1,0:T(1,128)S(1)}, u32[]{:S(2)}, u32[]{:S(2)}) async-start(f32[128,1,6272]{2,1,0:T(1,128)} %bitcast.8), calls=%async_computation | async-start | bytes 6422528 | tf_op jit(solution)/shard_map/all_to_all | solution.py:366
  16.7 4.2 %shard_map.69.book_hbm = bf16[32,256,256]{2,1,0:T(8,128)(2,1)} custom-call(f32[6,32,256]{2,1,0:T(8,128)} %bitcast.9), custom_call_target="tpu_custom_call" | custom-call | flops 268435456 | bytes 5242880 | tf_op jit(solution)/shard_map/pallas_call | solution.py:400
  20.8 1.9 %shard_map.72 = (f32[192,128]{1,0:T(8,128)}, f32[192,128]{1,0:T(8,128)}, f32[192,128]{1,0:T(8,128)}, f32[192,128]{1,0:T(8,128)}) custom-call(s32[1]{0:T(128)} %bitcast.rep_ref, f32[128,768]{1,0:T(8,128)} %old_ref), custom_call_target="tpu_custom_call" | custom-call | flops 1048576 | bytes 1048576 | tf_op jit(solution)/shard_map/pallas_call | solution.py:405
  22.7 0.0 copy-start.1
  22.7 1.5 %collective-permute-start.3 = (f32[192,128]{1,0:T(8,128)}, f32[192,128]{1,0:T(8,128)S(1)}, u32[]{:S(2)}, u32[]{:S(2)}) collective-permute-start(f32[192,128]{1,0:T(8,128)} %get-tuple-element.23), channel_id=1, source_target_pairs={{0,1},{1,2},{2,3},{3,0},{4,5},{5,6},{6,7},{7,4},{8,9},{9,10},{10,1... | collective-permute-start | bytes 294920 | tf_op jit(solution)/shard_map/ppermute | solution.py:410
  24.2 2.9 %collective-permute-start.4 = (f32[192,128]{1,0:T(8,128)}, f32[192,128]{1,0:T(8,128)S(1)}, u32[]{:S(2)}, u32[]{:S(2)}) collective-permute-start(f32[192,128]{1,0:T(8,128)} %get-tuple-element.24), channel_id=1, source_target_pairs={{0,2},{1,3},{2,0},{3,1},{4,6},{5,7},{6,4},{7,5},{8,10},{9,11},{10,... | collective-permute-start | bytes 294920 | tf_op jit(solution)/shard_map/ppermute | solution.py:410
  27.2 0.9 %collective-permute-start.5 = (f32[192,128]{1,0:T(8,128)}, f32[192,128]{1,0:T(8,128)}, u32[]{:S(2)}, u32[]{:S(2)}) collective-permute-start(f32[192,128]{1,0:T(8,128)} %get-tuple-element.25), channel_id=1, source_target_pairs={{0,3},{1,0},{2,1},{3,2},{4,7},{5,4},{6,5},{7,6},{8,11},{9,8},{10,9... | collective-permute-start | bytes 294920 | tf_op jit(solution)/shard_map/ppermute | solution.py:410
  28.1 31.3 %all-to-all-done = f32[128,1,6272]{2,1,0:T(1,128)S(1)} async-done(((f32[128,1,6272]{2,1,0:T(1,128)}), f32[128,1,6272]{2,1,0:T(1,128)S(1)}, u32[]{:S(2)}, u32[]{:S(2)}) %all-to-all-start) | async-done | bytes 3211296 | tf_op jit(solution)/shard_map/all_to_all | solution.py:366
  59.4 1.2 %shard_map.70 = (f32[4,200,128]{2,1,0:T(8,128)S(1)}, f32[200,128]{1,0:T(8,128)S(1)}, f32[200,128]{1,0:T(8,128)S(1)}, f32[200,128]{1,0:T(8,128)S(1)}) custom-call(s32[1]{0:T(128)} %bitcast.rep_ref, f32[6272,128]{1,0:T(8,128)S(1)} %bitcast.6), custom_call_target="tpu_custom_call" | custom-call | flops 268435456 | bytes 4194304 | tf_op jit(solution)/shard_map/pallas_call | solution.py:414
  60.6 0.6 collective-permute-start
  61.3 0.6 collective-permute-start.1
  61.9 0.0 collective-permute-done.3.one_hbm
  61.9 1.9 %collective-permute-start.2 = (f32[200,128]{1,0:T(8,128)S(1)}, f32[200,128]{1,0:T(8,128)S(1)}, u32[]{:S(2)}, u32[]{:S(2)}) collective-permute-start(f32[200,128]{1,0:T(8,128)S(1)} %get-tuple-element.19), channel_id=1, source_target_pairs={{0,3},{1,0},{2,1},{3,2},{4,7},{5,4},{6,5},{7,6},{8,11},{9,8},{10,9... | collective-permute-start | bytes 307208 | tf_op jit(solution)/shard_map/ppermute | solution.py:424
  63.7 0.0 collective-permute-done.4.two_hbm
  63.7 0.0 collective-permute-done.5.three_hbm
  63.8 0.0 copy-done.1
  63.8 0.0 copy-start
  63.8 21.8 %shard_map.73 = f32[32,4096]{1,0:T(8,128)} custom-call(s32[1]{0:T(128)} %bitcast.rep_ref, f32[6272,128]{1,0:T(8,128)S(1)} %bitcast.7, f32[4,200,128]{2,1,0:T(8,128)S(1)} %get-tuple-element.16.own_hbm.sums_hbm, bf16[32,256,256]{2,1,0:T(8,128)(2,1)} %shard_map.69.book_hbm, f32[192,128]{1,0:T(8,128)S(1)} %copy-done.1, ...), custom_call_target="tpu_custom_call" | custom-call | flops 4294967296 | bytes 8388608 | tf_op jit(solution)/shard_map/pallas_call | solution.py:372
  85.6 0.0 collective-permute-done.one_hbm
  85.6 0.0 collective-permute-done.1.two_hbm
  85.6 0.0 collective-permute-done.2.three_hbm
  85.6 0.0 copy-done
  85.6 1.7 %shard_map.71 = f32[128,768]{1,0:T(8,128)} custom-call(s32[1]{0:T(128)} %bitcast.rep_ref, f32[4,200,128]{2,1,0:T(8,128)S(1)} %get-tuple-element.16.own_hbm.sums_hbm, f32[200,128]{1,0:T(8,128)S(1)} %collective-permute-done.one_hbm, f32[200,128]{1,0:T(8,128)S(1)} %collective-permute-done.1.two_hbm, f32[200,128]{1,0:T(8,128)S(1)} %collective-permute-done.2.three_hbm, ...), custom_call_target="tpu_custom_call" | custom-call | flops 262144 | bytes 1048576 | tf_op jit(solution)/shard_map/pallas_call | solution.py:427
Async XLA Ops:
  5.1 54.3 %all-to-all-start = ((f32[128,1,6272]{2,1,0:T(1,128)}), f32[128,1,6272]{2,1,0:T(1,128)S(1)}, u32[]{:S(2)}, u32[]{:S(2)}) async-start(f32[128,1,6272]{2,1,0:T(1,128)} %bitcast.8), calls=%async_computation | async-start | bytes 6422528 | tf_op jit(solution)/shard_map/all_to_all | solution.py:366
  22.7 41.0 %copy-start.1 = (f32[192,128]{1,0:T(8,128)S(1)}, f32[192,128]{1,0:T(8,128)}, u32[]{:S(2)}) copy-start(f32[192,128]{1,0:T(8,128)} %get-tuple-element.22.own_hbm) | copy-start | bytes 294916
  22.7 39.1 %collective-permute-start.3 = (f32[192,128]{1,0:T(8,128)}, f32[192,128]{1,0:T(8,128)S(1)}, u32[]{:S(2)}, u32[]{:S(2)}) collective-permute-start(f32[192,128]{1,0:T(8,128)} %get-tuple-element.23), channel_id=1, source_target_pairs={{0,1},{1,2},{2,3},{3,0},{4,5},{5,6},{6,7},{7,4},{8,9},{9,10},{10,1... | collective-permute-start | bytes 294920 | tf_op jit(solution)/shard_map/ppermute | solution.py:410
  24.2 39.5 %collective-permute-start.4 = (f32[192,128]{1,0:T(8,128)}, f32[192,128]{1,0:T(8,128)S(1)}, u32[]{:S(2)}, u32[]{:S(2)}) collective-permute-start(f32[192,128]{1,0:T(8,128)} %get-tuple-element.24), channel_id=1, source_target_pairs={{0,2},{1,3},{2,0},{3,1},{4,6},{5,7},{6,4},{7,5},{8,10},{9,11},{10,... | collective-permute-start | bytes 294920 | tf_op jit(solution)/shard_map/ppermute | solution.py:410
  27.2 36.6 %collective-permute-start.5 = (f32[192,128]{1,0:T(8,128)}, f32[192,128]{1,0:T(8,128)}, u32[]{:S(2)}, u32[]{:S(2)}) collective-permute-start(f32[192,128]{1,0:T(8,128)} %get-tuple-element.25), channel_id=1, source_target_pairs={{0,3},{1,0},{2,1},{3,2},{4,7},{5,4},{6,5},{7,6},{8,11},{9,8},{10,9... | collective-permute-start | bytes 294920 | tf_op jit(solution)/shard_map/ppermute | solution.py:410
  60.6 24.9 %collective-permute-start = (f32[200,128]{1,0:T(8,128)S(1)}, f32[200,128]{1,0:T(8,128)S(1)}, u32[]{:S(2)}, u32[]{:S(2)}) collective-permute-start(f32[200,128]{1,0:T(8,128)S(1)} %get-tuple-element.17), channel_id=1, source_target_pairs={{0,1},{1,2},{2,3},{3,0},{4,5},{5,6},{6,7},{7,4},{8,9},{9,10},{10,1... | collective-permute-start | bytes 307208 | tf_op jit(solution)/shard_map/ppermute | solution.py:424
  61.3 24.3 %collective-permute-start.1 = (f32[200,128]{1,0:T(8,128)S(1)}, f32[200,128]{1,0:T(8,128)S(1)}, u32[]{:S(2)}, u32[]{:S(2)}) collective-permute-start(f32[200,128]{1,0:T(8,128)S(1)} %get-tuple-element.18), channel_id=1, source_target_pairs={{0,2},{1,3},{2,0},{3,1},{4,6},{5,7},{6,4},{7,5},{8,10},{9,11},{10,... | collective-permute-start | bytes 307208 | tf_op jit(solution)/shard_map/ppermute | solution.py:424
  61.9 23.7 %collective-permute-start.2 = (f32[200,128]{1,0:T(8,128)S(1)}, f32[200,128]{1,0:T(8,128)S(1)}, u32[]{:S(2)}, u32[]{:S(2)}) collective-permute-start(f32[200,128]{1,0:T(8,128)S(1)} %get-tuple-element.19), channel_id=1, source_target_pairs={{0,3},{1,0},{2,1},{3,2},{4,7},{5,4},{6,5},{7,6},{8,11},{9,8},{10,9... | collective-permute-start | bytes 307208 | tf_op jit(solution)/shard_map/ppermute | solution.py:424
  63.8 21.8 %copy-start = (f32[128,768]{1,0:T(8,128)S(1)}, f32[128,768]{1,0:T(8,128)}, u32[]{:S(2)}) copy-start(f32[128,768]{1,0:T(8,128)} %old_ref) | copy-start | bytes 1179652

commit v6 on v5

--- a/solution.py
+++ b/solution.py
@@ -401,7 +401,6 @@
         book_kernel, shape(32, 256, 256, dtype=BF16), [VMEM], VMEM, flops=2**28, moved=5 * 2**20
     )(jnp.transpose(codebook, (2, 0, 1)))
 
-    old_centroids, book = lax.optimization_barrier((old_centroids, book))
     quarters = call(
         quarters_kernel, [shape(192, 128)] * 4, [SMEM, VMEM], [VMEM] * 4, flops=2**20, moved=2**20
     )(rep, old_centroids)

time: 87.8 us -> 87.8 us (level)
  no operation moved by 1% of the time
where the time goes in v6:
time: 87.8 us; the launch traced here: 87.5 us
  Pallas kernels  35.3 us (40%)
  waiting for transfers between devices  31.3 us (36%)
  starting transfers between devices  20 us (23%)
  between operations  0.89 us (1%)
    all_to_all x1, waiting for transfers between devices, exchange(): lax.all_to_all(outgoing.reshape(128, 1, message * 128), ('shard', 'rep'),...  31.3 us
    pallas_call x1, Pallas kernels, score_call(): call(score_kernel, shape(32, 4096), [SMEM, VMEM] + [HBM] * 6, HBM, [pltpu...  21.8 us
    all_to_all x1, starting transfers between devices, exchange(): lax.all_to_all(outgoing.reshape(128, 1, message * 128), ('shard', 'rep'),...  11.5 us
    ppermute x3, starting transfers between devices, local(): lax.ppermute(quarters[step], 'rep', [(i, (i + step) % 4) for i in range(4)])  5.35 us
    pallas_call x1, Pallas kernels, pack_call(): call(functools.partial(pack_kernel, chunk, parts), shape(128 * message, 1...  4.5 us
    pallas_call x1, Pallas kernels, local(): call(book_kernel, shape(32, 256, 256, dtype=BF16), [VMEM], VMEM, flops=2...  4.19 us
    ppermute x3, starting transfers between devices, local(): lax.ppermute(sent[step - 1], 'rep', [(i, (i + step) % 4) for i in range(4)])  3.11 us
    pallas_call x1, Pallas kernels, local(): call(quarters_kernel, [shape(192, 128)] * 4, [SMEM, VMEM], [VMEM] * 4, fl...  1.93 us
  transfers between devices with their start and end apart: 7, of which 1 were waited for; matrix products, arithmetic and copies ran while one was open for 0% of the time, Pallas kernels for 33%

profile of v6, /device:TPU:1, one launch (start us, length us, event | category | flops | bytes accessed | tf_op | source)
XLA Modules:
  0.0 87.5 jit_solution(240441472256136644)
XLA Ops:
  0.6 4.5 %shard_map.68 = f32[6272,128]{1,0:T(8,128)} custom-call(s32[1,512]{1,0:T(1,128)} %bitcast.10, s32[1,512]{1,0:T(1,128)} %bitcast.11, f32[512,768]{1,0:T(8,128)} %rows_hbm.1), custom_call_target="tpu_custom_call" | custom-call | flops 1610612736 | bytes 5242880 | tf_op jit(solution)/shard_map/pallas_call | solution.py:345
  5.1 11.5 %all-to-all-start = ((f32[128,1,6272]{2,1,0:T(1,128)}), f32[128,1,6272]{2,1,0:T(1,128)S(1)}, u32[]{:S(2)}, u32[]{:S(2)}) async-start(f32[128,1,6272]{2,1,0:T(1,128)} %bitcast.8), calls=%async_computation | async-start | bytes 6422528 | tf_op jit(solution)/shard_map/all_to_all | solution.py:366
  16.7 1.9 %shard_map.72 = (f32[192,128]{1,0:T(8,128)}, f32[192,128]{1,0:T(8,128)}, f32[192,128]{1,0:T(8,128)}, f32[192,128]{1,0:T(8,128)}) custom-call(s32[1]{0:T(128)} %bitcast.rep_ref, f32[128,768]{1,0:T(8,128)} %old_ref.1), custom_call_target="tpu_custom_call" | custom-call | flops 1048576 | bytes 1048576 | tf_op jit(solution)/shard_map/pallas_call | solution.py:404
  18.6 1.5 %collective-permute-start.3 = (f32[192,128]{1,0:T(8,128)}, f32[192,128]{1,0:T(8,128)S(1)}, u32[]{:S(2)}, u32[]{:S(2)}) collective-permute-start(f32[192,128]{1,0:T(8,128)} %get-tuple-element.19), channel_id=1, source_target_pairs={{0,1},{1,2},{2,3},{3,0},{4,5},{5,6},{6,7},{7,4},{8,9},{9,10},{10,1... | collective-permute-start | bytes 294920 | tf_op jit(solution)/shard_map/ppermute | solution.py:409
  20.1 2.9 %collective-permute-start.4 = (f32[192,128]{1,0:T(8,128)}, f32[192,128]{1,0:T(8,128)S(1)}, u32[]{:S(2)}, u32[]{:S(2)}) collective-permute-start(f32[192,128]{1,0:T(8,128)} %get-tuple-element.20), channel_id=1, source_target_pairs={{0,2},{1,3},{2,0},{3,1},{4,6},{5,7},{6,4},{7,5},{8,10},{9,11},{10,... | collective-permute-start | bytes 294920 | tf_op jit(solution)/shard_map/ppermute | solution.py:409
  23.0 0.9 %collective-permute-start.5 = (f32[192,128]{1,0:T(8,128)}, f32[192,128]{1,0:T(8,128)}, u32[]{:S(2)}, u32[]{:S(2)}) collective-permute-start(f32[192,128]{1,0:T(8,128)} %get-tuple-element.21), channel_id=1, source_target_pairs={{0,3},{1,0},{2,1},{3,2},{4,7},{5,4},{6,5},{7,6},{8,11},{9,8},{10,9... | collective-permute-start | bytes 294920 | tf_op jit(solution)/shard_map/ppermute | solution.py:409
  23.9 0.0 copy-start.1
  23.9 4.2 %shard_map.69.book_hbm = bf16[32,256,256]{2,1,0:T(8,128)(2,1)} custom-call(f32[6,32,256]{2,1,0:T(8,128)} %bitcast.9), custom_call_target="tpu_custom_call" | custom-call | flops 268435456 | bytes 5242880 | tf_op jit(solution)/shard_map/pallas_call | solution.py:400
  28.1 31.3 %all-to-all-done = f32[128,1,6272]{2,1,0:T(1,128)S(1)} async-done(((f32[128,1,6272]{2,1,0:T(1,128)}), f32[128,1,6272]{2,1,0:T(1,128)S(1)}, u32[]{:S(2)}, u32[]{:S(2)}) %all-to-all-start) | async-done | bytes 3211296 | tf_op jit(solution)/shard_map/all_to_all | solution.py:366
  59.4 1.2 %shard_map.70 = (f32[4,200,128]{2,1,0:T(8,128)S(1)}, f32[200,128]{1,0:T(8,128)S(1)}, f32[200,128]{1,0:T(8,128)S(1)}, f32[200,128]{1,0:T(8,128)S(1)}) custom-call(s32[1]{0:T(128)} %bitcast.rep_ref, f32[6272,128]{1,0:T(8,128)S(1)} %bitcast.6), custom_call_target="tpu_custom_call" | custom-call | flops 268435456 | bytes 4194304 | tf_op jit(solution)/shard_map/pallas_call | solution.py:413
  60.6 0.6 collective-permute-start
  61.3 0.6 collective-permute-start.1
  61.9 0.0 collective-permute-done.3.one_hbm
  61.9 1.9 %collective-permute-start.2 = (f32[200,128]{1,0:T(8,128)S(1)}, f32[200,128]{1,0:T(8,128)S(1)}, u32[]{:S(2)}, u32[]{:S(2)}) collective-permute-start(f32[200,128]{1,0:T(8,128)S(1)} %get-tuple-element.16), channel_id=1, source_target_pairs={{0,3},{1,0},{2,1},{3,2},{4,7},{5,4},{6,5},{7,6},{8,11},{9,8},{10,9... | collective-permute-start | bytes 307208 | tf_op jit(solution)/shard_map/ppermute | solution.py:423
  63.7 0.0 collective-permute-done.4.two_hbm
  63.7 0.0 collective-permute-done.5.three_hbm
  63.8 0.0 copy-done.1
  63.8 0.0 copy-start
  63.8 21.8 %shard_map.73 = f32[32,4096]{1,0:T(8,128)} custom-call(s32[1]{0:T(128)} %bitcast.rep_ref, f32[6272,128]{1,0:T(8,128)S(1)} %bitcast.7, f32[4,200,128]{2,1,0:T(8,128)S(1)} %get-tuple-element.13.own_hbm.sums_hbm, bf16[32,256,256]{2,1,0:T(8,128)(2,1)} %shard_map.69.book_hbm, f32[192,128]{1,0:T(8,128)S(1)} %copy-done.1, ...), custom_call_target="tpu_custom_call" | custom-call | flops 4294967296 | bytes 8388608 | tf_op jit(solution)/shard_map/pallas_call | solution.py:372
  85.6 0.0 collective-permute-done.one_hbm
  85.6 0.0 collective-permute-done.1.two_hbm
  85.6 0.0 collective-permute-done.2.three_hbm
  85.6 0.0 copy-done
  85.6 1.7 %shard_map.71 = f32[128,768]{1,0:T(8,128)} custom-call(s32[1]{0:T(128)} %bitcast.rep_ref, f32[4,200,128]{2,1,0:T(8,128)S(1)} %get-tuple-element.13.own_hbm.sums_hbm, f32[200,128]{1,0:T(8,128)S(1)} %collective-permute-done.one_hbm, f32[200,128]{1,0:T(8,128)S(1)} %collective-permute-done.1.two_hbm, f32[200,128]{1,0:T(8,128)S(1)} %collective-permute-done.2.three_hbm, ...), custom_call_target="tpu_custom_call" | custom-call | flops 262144 | bytes 1048576 | tf_op jit(solution)/shard_map/pallas_call | solution.py:426
Async XLA Ops:
  5.1 54.3 %all-to-all-start = ((f32[128,1,6272]{2,1,0:T(1,128)}), f32[128,1,6272]{2,1,0:T(1,128)S(1)}, u32[]{:S(2)}, u32[]{:S(2)}) async-start(f32[128,1,6272]{2,1,0:T(1,128)} %bitcast.8), calls=%async_computation | async-start | bytes 6422528 | tf_op jit(solution)/shard_map/all_to_all | solution.py:366
  18.6 43.3 %collective-permute-start.3 = (f32[192,128]{1,0:T(8,128)}, f32[192,128]{1,0:T(8,128)S(1)}, u32[]{:S(2)}, u32[]{:S(2)}) collective-permute-start(f32[192,128]{1,0:T(8,128)} %get-tuple-element.19), channel_id=1, source_target_pairs={{0,1},{1,2},{2,3},{3,0},{4,5},{5,6},{6,7},{7,4},{8,9},{9,10},{10,1... | collective-permute-start | bytes 294920 | tf_op jit(solution)/shard_map/ppermute | solution.py:409
  20.1 43.7 %collective-permute-start.4 = (f32[192,128]{1,0:T(8,128)}, f32[192,128]{1,0:T(8,128)S(1)}, u32[]{:S(2)}, u32[]{:S(2)}) collective-permute-start(f32[192,128]{1,0:T(8,128)} %get-tuple-element.20), channel_id=1, source_target_pairs={{0,2},{1,3},{2,0},{3,1},{4,6},{5,7},{6,4},{7,5},{8,10},{9,11},{10,... | collective-permute-start | bytes 294920 | tf_op jit(solution)/shard_map/ppermute | solution.py:409
  23.0 40.7 %collective-permute-start.5 = (f32[192,128]{1,0:T(8,128)}, f32[192,128]{1,0:T(8,128)}, u32[]{:S(2)}, u32[]{:S(2)}) collective-permute-start(f32[192,128]{1,0:T(8,128)} %get-tuple-element.21), channel_id=1, source_target_pairs={{0,3},{1,0},{2,1},{3,2},{4,7},{5,4},{6,5},{7,6},{8,11},{9,8},{10,9... | collective-permute-start | bytes 294920 | tf_op jit(solution)/shard_map/ppermute | solution.py:409
  23.9 39.8 %copy-start.1 = (f32[192,128]{1,0:T(8,128)S(1)}, f32[192,128]{1,0:T(8,128)}, u32[]{:S(2)}) copy-start(f32[192,128]{1,0:T(8,128)} %get-tuple-element.18.own_hbm) | copy-start | bytes 294916
  60.6 24.9 %collective-permute-start = (f32[200,128]{1,0:T(8,128)S(1)}, f32[200,128]{1,0:T(8,128)S(1)}, u32[]{:S(2)}, u32[]{:S(2)}) collective-permute-start(f32[200,128]{1,0:T(8,128)S(1)} %get-tuple-element.14), channel_id=1, source_target_pairs={{0,1},{1,2},{2,3},{3,0},{4,5},{5,6},{6,7},{7,4},{8,9},{9,10},{10,1... | collective-permute-start | bytes 307208 | tf_op jit(solution)/shard_map/ppermute | solution.py:423
  61.3 24.3 %collective-permute-start.1 = (f32[200,128]{1,0:T(8,128)S(1)}, f32[200,128]{1,0:T(8,128)S(1)}, u32[]{:S(2)}, u32[]{:S(2)}) collective-permute-start(f32[200,128]{1,0:T(8,128)S(1)} %get-tuple-element.15), channel_id=1, source_target_pairs={{0,2},{1,3},{2,0},{3,1},{4,6},{5,7},{6,4},{7,5},{8,10},{9,11},{10,... | collective-permute-start | bytes 307208 | tf_op jit(solution)/shard_map/ppermute | solution.py:423
  61.9 23.7 %collective-permute-start.2 = (f32[200,128]{1,0:T(8,128)S(1)}, f32[200,128]{1,0:T(8,128)S(1)}, u32[]{:S(2)}, u32[]{:S(2)}) collective-permute-start(f32[200,128]{1,0:T(8,128)S(1)} %get-tuple-element.16), channel_id=1, source_target_pairs={{0,3},{1,0},{2,1},{3,2},{4,7},{5,4},{6,5},{7,6},{8,11},{9,8},{10,9... | collective-permute-start | bytes 307208 | tf_op jit(solution)/shard_map/ppermute | solution.py:423
  63.8 21.8 %copy-start = (f32[128,768]{1,0:T(8,128)S(1)}, f32[128,768]{1,0:T(8,128)}, u32[]{:S(2)}) copy-start(f32[128,768]{1,0:T(8,128)} %old_ref.1) | copy-start | bytes 1179652
